TPU v7x, 256 devices: a whole 4x4x8 slice. The times are simulated.
256 devices in a mesh: context: 32 (over z, x), tensor: 8 (over y, core).
Axes of the slice: x: 4, y: 4, z: 8, core: 2. Of those that a mesh axis runs over, the one named last changes fastest.
Arguments:
- query_proj: bfloat16 [4096, 16384], P('tensor', 'context'), may hold values from -6 to 6
- key_proj: bfloat16 [4096, 16384], P('tensor', 'context'), may hold values from -6 to 6
- value_proj: bfloat16 [4096, 16384], P('tensor', 'context'), may hold values from -6 to 6
- short_weight: float32 [3, 3, 4096], P(None, None, 'tensor'), may hold values from -3 to 3
- skip_bias: float32 [4096], P('tensor'), may hold values from -4 to 4
- filter_taps: float32 [8, 16384], P('tensor', 'context'), may hold values from -1.4 to 1.4
Outputs:
- mixed: bfloat16 [4096, 16384], P('tensor', 'context')
All inputs are finite; a program needn't handle non-finite values.
Results may differ from a plain program's by a relative error of at most 0.001.
Values may be sent and summed in bfloat16 or wider, within the bound.
No kernel may reach another device: no remote copies, remote signals or barrier semaphores. Data moves between devices by JAX's collectives and lax.ppermute only.
A program may use at most 128 MiB of HBM per device.

v0:
```python
import math

import jax
import jax.numpy as jnp
from jax import lax
from jax.sharding import PartitionSpec as P

FILT = 8
RADIX = 128


def swapped(value, axis, apart):
    mask = 2**apart
    pairs = [(source, source ^ mask) for source in range(lax.axis_size(axis))]
    return lax.ppermute(value, axis, pairs)


def from_behind(array, axis, by):
    count = lax.axis_size(axis)
    pairs = [(i, i + by) for i in range(count) if 0 <= i + by < count]
    return lax.ppermute(array, axis, pairs)


def reversed_bits(number, bit_count):
    summed = jnp.zeros_like(number)
    for bit_pos in range(bit_count):
        summed = summed + (number >> bit_pos & 1) * (1 << bit_count - 1 - bit_pos)
    return summed


def rotate_by(values, cos_part, sin_part):
    return jnp.stack(
        [values[0] * cos_part - values[1] * sin_part, values[0] * sin_part + values[1] * cos_part]
    )


def dft_matrix(length, direction):
    counter = jnp.arange(length, dtype=jnp.int32)
    product = counter[:, None] * counter[None, :] % length
    angles = direction * 2.0 * math.pi * product.astype(jnp.float32) / length
    return (jnp.cos(angles), jnp.sin(angles))


def inner_twiddle(first_len, second_len, direction):
    product = (
        jnp.arange(first_len, dtype=jnp.int32)[:, None]
        * jnp.arange(second_len, dtype=jnp.int32)[None, :]
    )
    angles = direction * 2.0 * math.pi * product.astype(jnp.float32) / (first_len * second_len)
    return (jnp.cos(angles), jnp.sin(angles))


def left_apply(matrix, values):
    real_mat, imag_mat = matrix
    form = "ab,...bk->...ak"
    highest = lax.Precision.HIGHEST
    real_out = jnp.einsum(form, real_mat, values[0], precision=highest) - jnp.einsum(
        form, imag_mat, values[1], precision=highest
    )
    imag_out = jnp.einsum(form, real_mat, values[1], precision=highest) + jnp.einsum(
        form, imag_mat, values[0], precision=highest
    )
    return jnp.stack([real_out, imag_out])


def right_apply(values, matrix):
    real_mat, imag_mat = matrix
    form = "...jb,bk->...jk"
    highest = lax.Precision.HIGHEST
    real_out = jnp.einsum(form, values[0], real_mat, precision=highest) - jnp.einsum(
        form, values[1], imag_mat, precision=highest
    )
    imag_out = jnp.einsum(form, values[1], real_mat, precision=highest) + jnp.einsum(
        form, values[0], imag_mat, precision=highest
    )
    return jnp.stack([real_out, imag_out])


def local_forward(values):
    dims_in = values.shape
    second = dims_in[-1] // RADIX
    blocks = values.reshape(dims_in[:-1] + (RADIX, second))
    blocks = left_apply(dft_matrix(RADIX, -1.0), blocks)
    cos_part, sin_part = inner_twiddle(RADIX, second, -1.0)
    blocks = rotate_by(blocks, cos_part, sin_part)
    return right_apply(blocks, dft_matrix(second, -1.0))


def local_inverse(spectra):
    dims_in = spectra.shape
    second = dims_in[-1]
    blocks = right_apply(spectra, dft_matrix(second, 1.0))
    cos_part, sin_part = inner_twiddle(RADIX, second, 1.0)
    blocks = rotate_by(blocks, cos_part, sin_part)
    blocks = left_apply(dft_matrix(RADIX, 1.0), blocks)
    return blocks.reshape(dims_in[:-2] + (RADIX * second,))


def cross_forward(values, position, bit_count):
    for level_bit in range(bit_count - 1, -1, -1):
        partner = swapped(values, "context", level_bit)
        half_span = 1 << level_bit
        is_upper = position >> level_bit & 1 == 1
        offset = (position & half_span - 1).astype(jnp.float32)
        sign_val = jnp.where(is_upper, -1.0, 1.0)
        combined = partner + sign_val * values
        angles = jnp.where(is_upper, -math.pi * offset / half_span, 0.0)
        values = rotate_by(combined, jnp.cos(angles), jnp.sin(angles))
    return values


def cross_inverse(values, position, bit_count):
    for level_bit in range(bit_count):
        partner = swapped(values, "context", level_bit)
        half_span = 1 << level_bit
        is_upper = position >> level_bit & 1 == 1
        offset = (position & half_span - 1).astype(jnp.float32)
        sign_val = jnp.where(is_upper, -1.0, 1.0)
        angles = math.pi * offset / half_span
        scaled = rotate_by(jnp.where(is_upper, values, partner), jnp.cos(angles), jnp.sin(angles))
        base_part = jnp.where(is_upper, partner, values)
        values = base_part + sign_val * scaled
    return values


def local(query_proj, key_proj, value_proj, short_weight, skip_bias, filter_taps):
    length = query_proj.shape[1]
    taps_count = short_weight.shape[1]
    ctx_count = lax.axis_size("context")
    bit_count = ctx_count.bit_length() - 1
    position = lax.axis_index("context")
    total_len = length * ctx_count
    streams = jnp.stack([query_proj, key_proj, value_proj])
    rim_cols = streams[:, :, length - (taps_count - 1) :]
    before = from_behind(rim_cols, "context", 1)
    extended = jnp.concatenate([before, streams], axis=2).astype(jnp.float32)
    shorted = short_weight[:, 0, :, None] * extended[:, :, taps_count - 1 :]
    for lag_step in range(1, taps_count):
        start_col = taps_count - 1 - lag_step
        shorted = (
            shorted
            + short_weight[:, lag_step, :, None] * extended[:, :, start_col : start_col + length]
        )
    query_short = shorted[0]
    product_in = shorted[1] * shorted[2]
    signal_imag = jnp.zeros_like(product_in)
    signal_rows = product_in.shape[0]
    global_pos = position * length + jnp.arange(length, dtype=jnp.int32)
    theta = math.pi * global_pos.astype(jnp.float32) / total_len
    cos_n = jnp.cos(theta)
    sin_n = jnp.sin(theta)
    real_rows = jnp.concatenate([product_in, filter_taps], axis=0)
    imag_rows = jnp.concatenate([signal_imag, jnp.zeros_like(filter_taps)], axis=0)
    modulated_real = real_rows * cos_n + imag_rows * sin_n
    modulated_imag = imag_rows * cos_n - real_rows * sin_n
    values = jnp.stack(
        [jnp.stack([real_rows, modulated_real]), jnp.stack([imag_rows, modulated_imag])]
    )
    values = cross_forward(values, position, bit_count)
    freq_class = reversed_bits(position, bit_count)
    phase_int = jnp.arange(length, dtype=jnp.int32) * freq_class
    phase = 2.0 * math.pi * phase_int.astype(jnp.float32) / total_len
    cos_phase = jnp.cos(phase)
    sin_phase = jnp.sin(phase)
    values = rotate_by(values, cos_phase, -sin_phase)
    spectra = local_forward(values)
    signal_spec = spectra[:, :, :signal_rows]
    filt_spec = spectra[:, :, signal_rows:]
    filt_spec = lax.all_gather(filt_spec, "tensor", axis=2, tiled=True)
    tail_dims = signal_spec.shape[3:]
    grouped = signal_spec.reshape((2, 2, signal_rows // FILT, FILT) + tail_dims)
    filt_real = filt_spec[0][:, None]
    filt_imag = filt_spec[1][:, None]
    prod_real = grouped[0] * filt_real - grouped[1] * filt_imag
    prod_imag = grouped[0] * filt_imag + grouped[1] * filt_real
    filtered = jnp.stack([prod_real, prod_imag]).reshape((2, 2, signal_rows) + tail_dims)
    restored = local_inverse(filtered)
    restored = rotate_by(restored, cos_phase, sin_phase)
    restored = cross_inverse(restored, position, bit_count)
    scale_back = 2.0 * total_len
    out_real = (restored[0, 0] + restored[0, 1] * cos_n - restored[1, 1] * sin_n) / scale_back
    mixed = query_short * (out_real + skip_bias[:, None] * product_in)
    return mixed.astype(jnp.bfloat16)


def solution(mesh):
    in_specs = (
        P("tensor", "context"),
        P("tensor", "context"),
        P("tensor", "context"),
        P(None, None, "tensor"),
        P("tensor"),
        P("tensor", "context"),
    )
    out_specs = P("tensor", "context")
    return jax.shard_map(local, mesh=mesh, in_specs=in_specs, out_specs=out_specs, check_vma=False)
```

profile of v0, /device:TPU:8, one launch (start us, length us, event | category | flops | bytes accessed | tf_op | source)
XLA Modules:
  0.0 1536.1 jit_solution(12880283083862841627)
XLA Ops:
  5.8 7.3 collective-permute-done
  21.2 5.2 copy.100
  26.4 11.7 collective-permute-start.1
  38.3 181.6 %collective-permute-done.1 = f32[2,2,513,512]{3,1,2,0:T(2,128)} collective-permute-done((f32[2,2,513,512]{3,1,2,0:T(2,128)}, f32[2,2,513,512]{3,1,2,0:T(2,128)}, u32[]{:S(2)}, u32[]{:S(2)}) %collective-permute-start.1) | collective-permute-done | bytes 4202528 | tf_op jit(solution)/shard_map/ppermute | solution.py:15
  226.1 5.2 copy.102
  231.5 181.5 %collective-permute-done.2 = f32[2,2,513,512]{3,1,2,0:T(2,128)} collective-permute-done((f32[2,2,513,512]{3,1,2,0:T(2,128)}, f32[2,2,513,512]{3,1,2,0:T(2,128)}, u32[]{:S(2)}, u32[]{:S(2)}) %collective-permute-start.2) | collective-permute-done | bytes 4202528 | tf_op jit(solution)/shard_map/ppermute | solution.py:15
  419.2 5.2 copy.104
  425.1 92.8 %collective-permute-done.3 = f32[2,2,513,512]{3,1,2,0:T(2,128)} collective-permute-done((f32[2,2,513,512]{3,1,2,0:T(2,128)}, f32[2,2,513,512]{3,1,2,0:T(2,128)}, u32[]{:S(2)}, u32[]{:S(2)}) %collective-permute-start.3) | collective-permute-done | bytes 4202528 | tf_op jit(solution)/shard_map/ppermute | solution.py:15
  524.1 5.2 copy.106
  529.5 93.5 %collective-permute-done.4 = f32[2,2,513,512]{3,1,2,0:T(2,128)} collective-permute-done((f32[2,2,513,512]{3,1,2,0:T(2,128)}, f32[2,2,513,512]{3,1,2,0:T(2,128)}, u32[]{:S(2)}, u32[]{:S(2)}) %collective-permute-start.4) | collective-permute-done | bytes 4202528 | tf_op jit(solution)/shard_map/ppermute | solution.py:15
  629.2 5.2 copy.108
  635.2 90.6 %collective-permute-done.5 = f32[2,2,513,512]{3,1,2,0:T(2,128)} collective-permute-done((f32[2,2,513,512]{3,1,2,0:T(2,128)}, f32[2,2,513,512]{3,1,2,0:T(2,128)}, u32[]{:S(2)}, u32[]{:S(2)}) %collective-permute-start.5) | collective-permute-done | bytes 4202528 | tf_op jit(solution)/shard_map/ppermute | solution.py:15
  736.2 4.8 copy.110
  741.0 6.1 multiply_subtract_fusion
  754.4 5.0 copy.115
  768.1 4.1 fusion.19
  776.1 4.2 subtract_bitcast_fusion
  780.3 4.1 add_bitcast_fusion
  784.4 11.7 all_gather.3
  806.7 4.1 convolution_subtract_fusion.1
  810.8 5.1 multiply_subtract_fusion.12
  827.0 4.4 copy.125
  843.3 92.5 %collective-permute-done.6 = f32[2,2,512,512]{3,2,1,0:T(8,128)S(1)} collective-permute-done((f32[2,2,512,512]{3,2,1,0:T(8,128)S(1)}, f32[2,2,512,512]{3,2,1,0:T(8,128)S(1)}, u32[]{:S(2)}, u32[]{:S(2)}) %collective-permute-start.6) | collective-permute-done | bytes 4194336 | tf_op jit(solution)/shard_map/ppermute | solution.py:15
  942.5 93.1 %collective-permute-done.7 = f32[2,2,512,512]{3,2,1,0:T(8,128)} collective-permute-done((f32[2,2,512,512]{3,2,1,0:T(8,128)}, f32[2,2,512,512]{3,2,1,0:T(8,128)}, u32[]{:S(2)}, u32[]{:S(2)}) %collective-permute-start.7) | collective-permute-done | bytes 4194336 | tf_op jit(solution)/shard_map/ppermute | solution.py:15
  1035.6 5.4 broadcast_select_fusion.1
  1044.5 3.9 fusion.1
  1049.5 90.3 %collective-permute-done.8 = f32[2,2,512,512]{3,2,1,0:T(8,128)} collective-permute-done((f32[2,2,512,512]{3,2,1,0:T(8,128)}, f32[2,2,512,512]{3,2,1,0:T(8,128)}, u32[]{:S(2)}, u32[]{:S(2)}) %collective-permute-start.8) | collective-permute-done | bytes 4194336 | tf_op jit(solution)/shard_map/ppermute | solution.py:15
  1143.7 5.8 fusion.2
  1150.8 179.9 %collective-permute-done.9 = f32[2,2,512,512]{3,2,1,0:T(8,128)} collective-permute-done((f32[2,2,512,512]{3,2,1,0:T(8,128)}, f32[2,2,512,512]{3,2,1,0:T(8,128)}, u32[]{:S(2)}, u32[]{:S(2)}) %collective-permute-start.9) | collective-permute-done | bytes 4194336 | tf_op jit(solution)/shard_map/ppermute | solution.py:15
  1334.6 5.8 fusion.3
  1343.9 182.6 %collective-permute-done.10 = f32[2,2,512,512]{3,2,1,0:T(8,128)} collective-permute-done((f32[2,2,512,512]{3,2,1,0:T(8,128)}, f32[2,2,512,512]{3,2,1,0:T(8,128)}, u32[]{:S(2)}, u32[]{:S(2)}) %collective-permute-start.10) | collective-permute-done | bytes 4194336 | tf_op jit(solution)/shard_map/ppermute | solution.py:15
  1530.4 3.9 fusion.4
  (133 shorter events, 131.1 us)
Async XLA Ops:
  0.0 13.1 copy-start.19
  0.0 13.1 copy-start.18
  0.0 13.1 copy-start.17
  1.3 11.8 collective-permute-start
  5.7 12.8 copy-start.20
  5.7 12.8 copy-start.22
  16.7 1.7 copy-start.4
  17.0 1.4 copy-start.24
  26.4 193.4 %collective-permute-start.1 = (f32[2,2,513,512]{3,1,2,0:T(2,128)}, f32[2,2,513,512]{3,1,2,0:T(2,128)}, u32[]{:S(2)}, u32[]{:S(2)}) collective-permute-start(f32[2,2,513,512]{3,1,2,0:T(2,128)} %copy.100), channel_id=1, source_target_pairs={{0,128},{8,136},{16,144},{24,152},{32,160},{40,168},{48,176},{56,1... | collective-permute-start | bytes 12607496 | tf_op jit(solution)/shard_map/ppermute | solution.py:15
  231.3 181.6 %collective-permute-start.2 = (f32[2,2,513,512]{3,1,2,0:T(2,128)}, f32[2,2,513,512]{3,1,2,0:T(2,128)}, u32[]{:S(2)}, u32[]{:S(2)}) collective-permute-start(f32[2,2,513,512]{3,1,2,0:T(2,128)} %copy.102), channel_id=1, source_target_pairs={{0,64},{8,72},{16,80},{24,88},{32,96},{40,104},{48,112},{56,120},{... | collective-permute-start | bytes 12607496 | tf_op jit(solution)/shard_map/ppermute | solution.py:15
  424.4 93.4 %collective-permute-start.3 = (f32[2,2,513,512]{3,1,2,0:T(2,128)}, f32[2,2,513,512]{3,1,2,0:T(2,128)}, u32[]{:S(2)}, u32[]{:S(2)}) collective-permute-start(f32[2,2,513,512]{3,1,2,0:T(2,128)} %copy.104), channel_id=1, source_target_pairs={{0,32},{8,40},{16,48},{24,56},{32,0},{40,8},{48,16},{56,24},{64,96... | collective-permute-start | bytes 12607496 | tf_op jit(solution)/shard_map/ppermute | solution.py:15
  529.3 93.6 %collective-permute-start.4 = (f32[2,2,513,512]{3,1,2,0:T(2,128)}, f32[2,2,513,512]{3,1,2,0:T(2,128)}, u32[]{:S(2)}, u32[]{:S(2)}) collective-permute-start(f32[2,2,513,512]{3,1,2,0:T(2,128)} %copy.106), channel_id=1, source_target_pairs={{0,16},{8,24},{16,0},{24,8},{32,48},{40,56},{48,32},{56,40},{64,80... | collective-permute-start | bytes 12607496 | tf_op jit(solution)/shard_map/ppermute | solution.py:15
  634.5 91.4 %collective-permute-start.5 = (f32[2,2,513,512]{3,1,2,0:T(2,128)}, f32[2,2,513,512]{3,1,2,0:T(2,128)}, u32[]{:S(2)}, u32[]{:S(2)}) collective-permute-start(f32[2,2,513,512]{3,1,2,0:T(2,128)} %copy.108), channel_id=1, source_target_pairs={{0,8},{8,0},{16,24},{24,16},{32,40},{40,32},{48,56},{56,48},{64,72... | collective-permute-start | bytes 12607496 | tf_op jit(solution)/shard_map/ppermute | solution.py:15
  759.4 3.9 copy-start.10
  759.4 3.9 copy-start.16
  842.4 95.3 %copy-start = (f32[1,2,512,512]{3,2,1,0:T(8,128)}, f32[1,2,512,512]{3,2,1,0:T(8,128)S(1)}, u32[]{:S(2)}) copy-start(f32[1,2,512,512]{3,2,1,0:T(8,128)S(1)} %get-tuple-element.22) | copy-start | bytes 6291460
  842.9 92.9 %collective-permute-start.6 = (f32[2,2,512,512]{3,2,1,0:T(8,128)S(1)}, f32[2,2,512,512]{3,2,1,0:T(8,128)S(1)}, u32[]{:S(2)}, u32[]{:S(2)}) collective-permute-start(f32[2,2,512,512]{3,2,1,0:T(8,128)S(1)} %pad_maximum_fusion.5), channel_id=1, source_target_pairs={{0,8},{8,0},{16,24},{24,16},{32,40},{40,32},{48,56},{56,48},{64,72... | collective-permute-start | bytes 12582920 | tf_op jit(solution)/shard_map/ppermute | solution.py:15
  935.8 2.3 copy-start.2
  937.6 4.2 copy-start.6
  937.6 4.2 copy-start.8
  941.8 93.8 %collective-permute-start.7 = (f32[2,2,512,512]{3,2,1,0:T(8,128)}, f32[2,2,512,512]{3,2,1,0:T(8,128)}, u32[]{:S(2)}, u32[]{:S(2)}) collective-permute-start(f32[2,2,512,512]{3,2,1,0:T(8,128)} %fusion), channel_id=1, source_target_pairs={{0,16},{8,24},{16,0},{24,8},{32,48},{40,56},{48,32},{56,40},{64,80... | collective-permute-start | bytes 12582920 | tf_op jit(solution)/shard_map/ppermute | solution.py:15
  1035.6 6.3 copy-start.9
  1041.1 1.6 copy-start.1
  1041.1 2.8 copy-start.3
  1041.1 3.4 copy-start.7
  1048.4 91.4 %collective-permute-start.8 = (f32[2,2,512,512]{3,2,1,0:T(8,128)}, f32[2,2,512,512]{3,2,1,0:T(8,128)}, u32[]{:S(2)}, u32[]{:S(2)}) collective-permute-start(f32[2,2,512,512]{3,2,1,0:T(8,128)} %fusion.1), channel_id=1, source_target_pairs={{0,32},{8,40},{16,48},{24,56},{32,0},{40,8},{48,16},{56,24},{64,96... | collective-permute-start | bytes 12582920 | tf_op jit(solution)/shard_map/ppermute | solution.py:15
  1149.5 181.3 %collective-permute-start.9 = (f32[2,2,512,512]{3,2,1,0:T(8,128)}, f32[2,2,512,512]{3,2,1,0:T(8,128)}, u32[]{:S(2)}, u32[]{:S(2)}) collective-permute-start(f32[2,2,512,512]{3,2,1,0:T(8,128)} %fusion.2), channel_id=1, source_target_pairs={{0,64},{8,72},{16,80},{24,88},{32,96},{40,104},{48,112},{56,120},{... | collective-permute-start | bytes 12582920 | tf_op jit(solution)/shard_map/ppermute | solution.py:15
  1340.4 186.2 %collective-permute-start.10 = (f32[2,2,512,512]{3,2,1,0:T(8,128)}, f32[2,2,512,512]{3,2,1,0:T(8,128)}, u32[]{:S(2)}, u32[]{:S(2)}) collective-permute-start(f32[2,2,512,512]{3,2,1,0:T(8,128)} %fusion.3), channel_id=1, source_target_pairs={{0,128},{8,136},{16,144},{24,152},{32,160},{40,168},{48,176},{56,1... | collective-permute-start | bytes 12582920 | tf_op jit(solution)/shard_map/ppermute | solution.py:15
  1530.4 4.0 copy-start.5
  1530.4 4.0 copy-start.21
  1530.4 4.0 copy-start.23
  1530.4 4.0 copy-start.25
  (5 other events, 6.7 us)
where the time goes:
time: 1540 us
  waiting for transfers between devices  1290 us (84%)
  other arithmetic  87.5 us (6%)
  local copies, waits for them, and re-layouts  68.8 us (4%)
  matrix products  57.3 us (4%)
  starting transfers between devices  22.2 us (1%)
    ppermute x10, waiting for transfers between devices, swapped(): return lax.ppermute(value, axis, pairs)  1280 us
  transfers between devices with their start and end apart: 11, of which 11 were waited for; matrix products, arithmetic and copies ran while one was open for 0% of the time, Pallas kernels for 0%

commit v1 on v0

v1 whole, which is shorter than its diff:
```python
import jax
import jax.numpy as jnp
from jax import lax
from jax.experimental import pallas as pl
from jax.experimental.pallas import tpu as pltpu
from jax.sharding import PartitionSpec as P

FILT = 8
TILE = 128
ROWS = 16
CHUNK = 72
GAIN = 16.0
SLOPE = 61.0
LIFT = 125.0
TINY = 1e-30
MIB = 1024 * 1024


def scale_of(peak):
    return jnp.maximum(peak, TINY).astype(jnp.bfloat16).astype(jnp.float32)


def encode(values, scale):
    level = jnp.log2(1.0 + jnp.abs(values) * (GAIN / scale))
    size = jnp.exp2(level * SLOPE - LIFT)
    return jnp.where(values < 0.0, -size, size)


def decode(codes, scale):
    level = (jnp.log2(jnp.abs(codes)) + LIFT) * (1.0 / SLOPE)
    size = (jnp.exp2(level) - 1.0) * (scale * (1.0 / GAIN))
    return jnp.where(codes < 0.0, -size, size)


def split(values):
    high = values.astype(jnp.bfloat16)
    low = (values - high.astype(jnp.float32)).astype(jnp.bfloat16)
    return high, low


def short_mix(stream, before, weights):
    length = stream.shape[1]
    lane = lax.broadcasted_iota(jnp.int32, stream.shape, 1)
    one = pltpu.roll(stream, 1, 1)
    one = jnp.where(lane == 0, before[:, 1:2], one)
    two = pltpu.roll(stream, 2, 1)
    two = jnp.where(lane == 0, before[:, 0:1], jnp.where(lane == 1, before[:, 1:2], two))
    return weights[0] * stream + weights[1] * one + weights[2] * two


def to_lanes(column):
    shape = (TILE, TILE)
    lane = lax.broadcasted_iota(jnp.int32, shape, 1)
    group = lax.broadcasted_iota(jnp.int32, shape, 0) // FILT
    spread = jnp.where(lane == group, column, 0.0)
    return spread.reshape(ROWS, FILT, TILE).sum(axis=0)


def front_kernel(key_ref, value_ref, side_ref, taps_ref, prod_ref, out_ref, coded):
    side = jnp.transpose(side_ref[...])
    key = key_ref[...].astype(jnp.float32)
    value = value_ref[...].astype(jnp.float32)
    key_short = short_mix(key, side[:, 10:12], [side[:, n : n + 1] for n in range(3, 6)])
    value_short = short_mix(value, side[:, 12:14], [side[:, n : n + 1] for n in range(6, 9)])
    product = key_short * value_short
    prod_ref[...] = product
    scale = scale_of(jnp.max(jnp.abs(product), axis=1, keepdims=True))
    coded_rows = encode(product, scale)
    for block in range(4):
        coded[block] = coded_rows[:, block * TILE : (block + 1) * TILE]
    scales = to_lanes(scale)
    row = lax.broadcasted_iota(jnp.int32, (8, TILE), 0)
    for filt in range(FILT):
        for block in range(4):
            part = coded[block, pl.ds(filt, ROWS, stride=FILT), :]
            out_ref[filt, pl.ds(block * ROWS, ROWS), :] = part.astype(jnp.bfloat16)
        taps = taps_ref[filt]
        tap_scale = scale_of(jnp.max(jnp.abs(taps)))
        tail = encode(taps, tap_scale)
        tail = jnp.where(row == 4, scales[filt : filt + 1, :], tail)
        tail = jnp.where(row == 5, tap_scale, tail)
        out_ref[filt, pl.ds(64, 8), :] = tail.astype(jnp.bfloat16)


def conv_kernel(in_ref, out_ref, high, low, taps, toep_high, toep_low, total):
    count = in_ref.shape[0]
    lane = lax.broadcasted_iota(jnp.int32, (ROWS, TILE), 1)
    row = lax.broadcasted_iota(jnp.int32, (ROWS, TILE), 0)

    def unpack(src, carry):
        tail = in_ref[src, pl.ds(64, 8), :].astype(jnp.float32)
        scale = jnp.sum(jnp.where(lane == row, tail[4:5, :], 0.0), axis=1, keepdims=True)
        taps[pl.ds(src * 4, 4), :] = decode(tail[0:4, :], tail[5:6, :])
        for block in range(4):
            part = in_ref[src, pl.ds(block * ROWS, ROWS), :].astype(jnp.float32)
            upper, lower = split(decode(part, scale))
            at = pl.ds(pl.multiple_of(src * 32 + (block // 2) * ROWS, ROWS), ROWS)
            cols = pl.ds((block % 2) * TILE, TILE)
            high[at, cols] = upper
            low[at, cols] = lower
        return carry

    lax.fori_loop(0, count, unpack, 0)
    wide_lane = lax.broadcasted_iota(jnp.int32, (TILE, TILE), 1)
    wide_row = lax.broadcasted_iota(jnp.int32, (TILE, TILE), 0)
    causal = wide_lane >= wide_row
    zero = jnp.zeros((TILE, TILE), jnp.bfloat16)
    toep_high[0] = zero
    toep_low[0] = zero

    def build(tile, before):
        line = jnp.broadcast_to(taps[pl.ds(tile, 1), :], (TILE, TILE))
        rolled = pltpu.roll(line, 0, 1, stride=1, stride_axis=0)
        upper, lower = split(jnp.where(causal, rolled, before))
        toep_high[tile + 1] = upper
        toep_low[tile + 1] = lower
        return rolled

    lax.fori_loop(0, count * 4, build, jnp.zeros((TILE, TILE), jnp.float32))
    blocks = count * 2
    size = blocks * ROWS

    def weight(ref, lag):
        top = jnp.concatenate([ref[2 * lag + 1], ref[2 * lag + 2]], axis=1)
        bottom = jnp.concatenate([ref[2 * lag], ref[2 * lag + 1]], axis=1)
        return jnp.concatenate([top, bottom], axis=0)

    for lag in range(blocks):
        rows = size - lag * ROWS
        upper = weight(toep_high, lag)
        lower = weight(toep_low, lag)
        left = jnp.concatenate([high[:rows, :], low[:rows, :], high[:rows, :]], axis=1)
        right = jnp.concatenate([upper, upper, lower], axis=0)
        part = jnp.dot(left, right, preferred_element_type=jnp.float32)
        if lag == 0:
            total[...] = part
        else:
            total[lag * ROWS :, :] += part

    pick = lax.broadcasted_iota(jnp.int32, (8, TILE), 0) == 0

    def pack(dst, carry):
        parts = []
        for block in range(4):
            at = pl.ds(pl.multiple_of(dst * 32 + (block // 2) * ROWS, ROWS), ROWS)
            parts.append(total[at, pl.ds((block % 2) * TILE, TILE)])
        peak = jnp.max(jnp.abs(parts[0]), axis=1, keepdims=True)
        for part in parts[1:]:
            peak = jnp.maximum(peak, jnp.max(jnp.abs(part), axis=1, keepdims=True))
        scale = scale_of(peak)
        for block in range(4):
            codes = encode(parts[block], scale).astype(jnp.bfloat16)
            out_ref[dst, pl.ds(block * ROWS, ROWS), :] = codes
        spread = jnp.sum(jnp.where(lane == row, scale, 0.0), axis=0, keepdims=True)
        out_ref[dst, pl.ds(64, 8), :] = jnp.where(pick, spread, 0.0).astype(jnp.bfloat16)
        return carry

    lax.fori_loop(0, count, pack, 0)


def back_kernel(in_ref, query_ref, side_ref, prod_ref, out_ref, plain):
    lane = lax.broadcasted_iota(jnp.int32, (ROWS, TILE), 1)
    row = lax.broadcasted_iota(jnp.int32, (ROWS, TILE), 0)
    for filt in range(FILT):
        tail = in_ref[filt, pl.ds(64, 8), :].astype(jnp.float32)
        scale = jnp.sum(jnp.where(lane == row, tail[0:1, :], 0.0), axis=1, keepdims=True)
        for block in range(4):
            part = in_ref[filt, pl.ds(block * ROWS, ROWS), :].astype(jnp.float32)
            plain[block, pl.ds(filt, ROWS, stride=FILT), :] = decode(part, scale)
    side = jnp.transpose(side_ref[...])
    query = query_ref[...].astype(jnp.float32)
    query_short = short_mix(query, side[:, 14:16], [side[:, n : n + 1] for n in range(3)])
    long = jnp.concatenate([plain[block] for block in range(4)], axis=1)
    mixed = query_short * (long + side[:, 9:10] * prod_ref[...])
    out_ref[...] = mixed.astype(jnp.bfloat16)


def front(key_proj, value_proj, side, taps):
    rows, length = key_proj.shape
    steps = rows // TILE
    stream = pl.BlockSpec((TILE, length), lambda n: (n, 0))
    return pl.pallas_call(
        front_kernel,
        grid=(steps,),
        in_specs=[
            stream,
            stream,
            pl.BlockSpec((16, TILE), lambda n: (0, n)),
            pl.BlockSpec((FILT, 8, TILE), lambda n: (0, 0, 0)),
        ],
        out_specs=[stream, pl.BlockSpec((FILT, CHUNK, TILE), lambda n: (n, 0, 0))],
        out_shape=[
            jax.ShapeDtypeStruct((rows, length), jnp.float32),
            jax.ShapeDtypeStruct((steps * FILT, CHUNK, TILE), jnp.bfloat16),
        ],
        scratch_shapes=[pltpu.VMEM((4, TILE, TILE), jnp.float32)],
        compiler_params=pltpu.CompilerParams(vmem_limit_bytes=16 * MIB),
        name="front",
    )(key_proj, value_proj, side, taps)


def conv(chunks):
    count = chunks.shape[0]
    size = count * 2 * ROWS
    whole = pl.BlockSpec(memory_space=pltpu.VMEM)
    return pl.pallas_call(
        conv_kernel,
        in_specs=[whole],
        out_specs=whole,
        out_shape=jax.ShapeDtypeStruct(chunks.shape, jnp.bfloat16),
        scratch_shapes=[
            pltpu.VMEM((size, 2 * TILE), jnp.bfloat16),
            pltpu.VMEM((size, 2 * TILE), jnp.bfloat16),
            pltpu.VMEM((count * 4, TILE), jnp.float32),
            pltpu.VMEM((count * 4 + 1, TILE, TILE), jnp.bfloat16),
            pltpu.VMEM((count * 4 + 1, TILE, TILE), jnp.bfloat16),
            pltpu.VMEM((size, 2 * TILE), jnp.float32),
        ],
        compiler_params=pltpu.CompilerParams(vmem_limit_bytes=40 * MIB),
        name="conv",
    )(chunks)


def back(chunks, query_proj, side, product):
    rows, length = query_proj.shape
    steps = rows // TILE
    stream = pl.BlockSpec((TILE, length), lambda n: (n, 0))
    return pl.pallas_call(
        back_kernel,
        grid=(steps,),
        in_specs=[
            pl.BlockSpec((FILT, CHUNK, TILE), lambda n: (n, 0, 0)),
            stream,
            pl.BlockSpec((16, TILE), lambda n: (0, n)),
            stream,
        ],
        out_specs=stream,
        out_shape=jax.ShapeDtypeStruct((rows, length), jnp.bfloat16),
        scratch_shapes=[pltpu.VMEM((4, TILE, TILE), jnp.float32)],
        compiler_params=pltpu.CompilerParams(vmem_limit_bytes=16 * MIB),
        name="back",
    )(chunks, query_proj, side, product)


def local(query_proj, key_proj, value_proj, short_weight, skip_bias, filter_taps):
    count = lax.axis_size("context")
    rows = query_proj.shape[0]
    rim = jnp.concatenate(
        [stream[:, -2:].T for stream in (key_proj, value_proj, query_proj)], axis=0
    )
    pairs = [(n, n + 1) for n in range(count - 1)]
    rim = lax.ppermute(rim, "context", pairs).astype(jnp.float32)
    side = jnp.concatenate([short_weight.reshape(9, rows), skip_bias[None, :], rim], axis=0)
    taps = jnp.pad(filter_taps.reshape(1, 4, TILE), ((0, 0), (0, 4), (0, 0)))
    taps = jnp.broadcast_to(taps, (FILT, 8, TILE))
    taps = lax.all_to_all(taps, "tensor", 0, 0, tiled=True)
    product, chunks = front(key_proj, value_proj, side, taps)
    chunks = lax.all_to_all(chunks, "context", 0, 0, tiled=True)
    chunks = conv(chunks)
    chunks = lax.all_to_all(chunks, "context", 0, 0, tiled=True)
    return back(chunks, query_proj, side, product)


def solution(mesh):
    in_specs = (
        P("tensor", "context"),
        P("tensor", "context"),
        P("tensor", "context"),
        P(None, None, "tensor"),
        P("tensor"),
        P("tensor", "context"),
    )
    out_specs = P("tensor", "context")
    return jax.shard_map(local, mesh=mesh, in_specs=in_specs, out_specs=out_specs, check_vma=False)
```

time: 1540 us -> 107 us (0.07)
  waiting for transfers between devices: 1290 us -> 3.27 us
  other arithmetic: 87.5 us -> 0.04 us
  local copies, waits for them, and re-layouts: 68.8 us -> 3.9 us
  matrix products: 57.3 us -> 0 us
  blocking collectives: 11.7 us -> 52.7 us
  Pallas kernels: 0 us -> 37.9 us
    ppermute x11 -> x1, waiting for transfers between devices: 1290 us -> 0.01 us  [local(): rim = lax.ppermute(rim, 'context', pairs).astype(jnp.float32)]
    dot_general x16 -> x0, matrix products: 57.3 us -> none  [the longest x2 9.24 us: right_apply(): jnp.einsum(form, values[0], imag_mat, precision=highest)]
    all_to_all x0 -> x2, blocking collectives: none -> 52.7 us  [local(): chunks = lax.all_to_all(chunks, 'context', 0, 0, tiled=True)]
    add x12 -> x0, other arithmetic: 45.3 us -> none  [the longest x5 23.1 us: cross_inverse(): values = base_part + sign_val * scaled]
    pallas_call x0 -> x3, Pallas kernels: none -> 37.9 us  [the longest x1 31.6 us: conv(): pl.pallas_call(conv_kernel, in_specs=[whole], out_specs=whole, out_shape=...]
    another operation x5 -> x0, local copies, waits for them, and re-layouts: 26.2 us -> none  [the longest x4 21 us: rotate_by(): jnp.stack([values[0] * cos_part - values[1] * sin_part, values[0] * sin_p...]
    sub x13 -> x0, other arithmetic: 18.9 us -> none  [the longest x12 17.3 us: rotate_by(): values[0] * cos_part - values[1] * sin_part]
    ppermute x11 -> x1, starting transfers between devices: 22.2 us -> 3.4 us  [local(): rim = lax.ppermute(rim, 'context', pairs).astype(jnp.float32)]
  transfers between devices with their start and end apart: 11 -> 2, of which waited for: 11 -> 1; matrix products, arithmetic and copies ran while one was open for 0% -> 1% of each run, Pallas kernels for 0% -> 0%
where the time goes in v1:
time: 107 us; the launch traced here: 106 us
  blocking collectives  52.7 us (49%)
  Pallas kernels  37.9 us (35%)
  starting transfers between devices  8.44 us (8%)
  local copies, waits for them, and re-layouts  3.9 us (4%)
  waiting for transfers between devices  3.27 us (3%)
    all_to_all x2, blocking collectives, local(): chunks = lax.all_to_all(chunks, 'context', 0, 0, tiled=True)  52.7 us
    pallas_call x1, Pallas kernels, conv(): pl.pallas_call(conv_kernel, in_specs=[whole], out_specs=whole, out_shape=...  31.6 us
    all_to_all x1, starting transfers between devices, local(): taps = lax.all_to_all(taps, 'tensor', 0, 0, tiled=True)  5.05 us
    pallas_call x1, Pallas kernels, front(): pl.pallas_call(front_kernel, grid=(steps,), in_specs=[stream, stream, pl....  3.77 us
    ppermute x1, starting transfers between devices, local(): rim = lax.ppermute(rim, 'context', pairs).astype(jnp.float32)  3.4 us
    all_to_all x1, waiting for transfers between devices, local(): taps = lax.all_to_all(taps, 'tensor', 0, 0, tiled=True)  3.26 us
    pallas_call x1, Pallas kernels, back(): pl.pallas_call(back_kernel, grid=(steps,), in_specs=[pl.BlockSpec((FILT,...  2.55 us
    slice x3, local copies, waits for them, and re-layouts, local(): stream[:, -2:]  2.26 us
  transfers between devices with their start and end apart: 2, of which 1 were waited for; matrix products, arithmetic and copies ran while one was open for 1% of the time, Pallas kernels for 0%

profile of v1, /device:TPU:8, one launch (start us, length us, event | category | flops | bytes accessed | tf_op | source)
XLA Modules:
  0.0 106.4 jit_solution(4472755107132725699)
XLA Ops:
  0.0 0.0 copy-start.1
  0.0 1.1 slice.11
  1.1 0.1 copy.12
  1.2 0.0 copy-start
  1.2 1.1 %slice.9 = bf16[512,2]{1,0:T(8,128)(2,1)S(1)} slice(bf16[512,512]{1,0:T(8,128)(2,1)} %key_ref.1), slice={[0:512], [510:512]} | slice | bytes 4096 | tf_op jit(solution)/shard_map/slice | solution.py:249
  2.3 0.1 copy.10
  2.4 0.0 copy-done.1
  2.4 0.1 slice.10
  2.5 0.1 copy.11
  2.6 0.0 copy-start.4
  2.6 3.4 %collective-permute-start = (bf16[6,512]{1,0:T(8,128)(2,1)S(1)}, bf16[6,512]{1,0:T(8,128)(2,1)S(1)}, u32[]{:S(2)}, u32[]{:S(2)}) collective-permute-start(bf16[6,512]{1,0:T(8,128)(2,1)S(1)} %pad_maximum_fusion.1), channel_id=1, source_target_pairs={{0,8},{8,16},{16,24},{24,32},{32,40},{40,48},{48,56},{56,64},{64,7... | collective-permute-start | bytes 18440 | tf_op jit(solution)/shard_map/ppermute | solution.py:252
  6.0 0.0 copy-done.4
  6.1 0.6 broadcast_in_dim.12
  6.7 0.0 copy-start.3
  6.7 5.0 %all-to-all-start = ((f32[8,8,128]{2,1,0:T(8,128)}), f32[8,8,128]{2,1,0:T(8,128)S(1)}, u32[]{:S(2)}, u32[]{:S(2)}) async-start(f32[8,8,128]{2,1,0:T(8,128)} %broadcast_in_dim.12), calls=%async_computation | async-start | bytes 65536 | tf_op jit(solution)/shard_map/all_to_all | solution.py:256
  11.7 0.0 copy-done.3
  11.8 0.0 collective-permute-done
  11.8 0.0 copy-start.5
  11.8 0.7 copy-done.5
  12.5 3.3 %all-to-all-done.taps_ref = f32[8,8,128]{2,1,0:T(8,128)S(1)} async-done(((f32[8,8,128]{2,1,0:T(8,128)}), f32[8,8,128]{2,1,0:T(8,128)S(1)}, u32[]{:S(2)}, u32[]{:S(2)}) %all-to-all-start) | async-done | bytes 32800 | tf_op jit(solution)/shard_map/all_to_all | solution.py:256
  15.7 0.0 copy-done
  15.7 3.8 %front.1 = (f32[512,512]{1,0:T(8,128)S(1)}, bf16[32,72,128]{2,1,0:T(8,128)(2,1)S(1)}) custom-call(bf16[512,512]{1,0:T(8,128)(2,1)S(1)} %copy-done, bf16[512,512]{1,0:T(8,128)(2,1)S(1)} %copy-done.1, f32[16,512]{1,0:T(8,128)S(1)} %pad_maximum_fusion.side_ref, f32[8,8,128]{2,1,0:T(8,128)S(1)} %all-to-all-done.taps_ref), custom_call_target="tpu_custom_call" | custom-call | tf_op jit(solution)/shard_map/front/pallas_call | solution.py:182
  19.5 29.7 %all_to_all.15.in_ref = bf16[32,72,128]{2,1,0:T(8,128)(2,1)S(1)} all-to-all(bf16[32,72,128]{2,1,0:T(8,128)(2,1)S(1)} %get-tuple-element.7), channel_id=1, replica_groups=mesh['context'=32,'tensor'=8] {'context'}, dimensions={0} | all-to-all | bytes 1179648 | tf_op jit(solution)/shard_map/all_to_all | solution.py:258
  49.2 31.6 %conv.1 = bf16[32,72,128]{2,1,0:T(8,128)(2,1)S(1)} custom-call(bf16[32,72,128]{2,1,0:T(8,128)(2,1)S(1)} %all_to_all.15.in_ref), custom_call_target="tpu_custom_call" | custom-call | tf_op jit(solution)/shard_map/conv/pallas_call | solution.py:206
  80.9 0.0 copy-start.2
  80.9 23.0 %all_to_all.16.in_ref = bf16[32,72,128]{2,1,0:T(8,128)(2,1)S(1)} all-to-all(bf16[32,72,128]{2,1,0:T(8,128)(2,1)S(1)} %conv.1), channel_id=1, replica_groups=mesh['context'=32,'tensor'=8] {'context'}, dimensions={0} | all-to-all | bytes 1179648 | tf_op jit(solution)/shard_map/all_to_all | solution.py:260
  103.9 0.0 copy-done.2
  103.9 2.5 %back.1 = bf16[512,512]{1,0:T(8,128)(2,1)} custom-call(bf16[32,72,128]{2,1,0:T(8,128)(2,1)S(1)} %all_to_all.16.in_ref, bf16[512,512]{1,0:T(8,128)(2,1)S(1)} %copy-done.2, f32[16,512]{1,0:T(8,128)S(1)} %pad_maximum_fusion.side_ref, f32[512,512]{1,0:T(8,128)S(1)} %get-tuple-element.8.prod_ref), custom_call_target="tpu_custom_call" | custom-call | tf_op jit(solution)/shard_map/back/pallas_call | solution.py:228
  (5 shorter events, 0.1 us)
Async XLA Ops:
  0.0 2.4 %copy-start.1 = (bf16[512,512]{1,0:T(8,128)(2,1)S(1)}, bf16[512,512]{1,0:T(8,128)(2,1)}, u32[]{:S(2)}) copy-start(bf16[512,512]{1,0:T(8,128)(2,1)} %value_ref.1) | copy-start | bytes 1572868
  1.2 14.6 %copy-start = (bf16[512,512]{1,0:T(8,128)(2,1)S(1)}, bf16[512,512]{1,0:T(8,128)(2,1)}, u32[]{:S(2)}) copy-start(bf16[512,512]{1,0:T(8,128)(2,1)} %key_ref.1) | copy-start | bytes 1572868
  2.6 3.4 %copy-start.4 = (f32[1,512]{1,0:T(1,128)S(1)}, f32[1,512]{1,0:T(1,128)}, u32[]{:S(2)}) copy-start(f32[1,512]{1,0:T(1,128)} %param.11) | copy-start | bytes 6148
  2.6 9.1 %collective-permute-start = (bf16[6,512]{1,0:T(8,128)(2,1)S(1)}, bf16[6,512]{1,0:T(8,128)(2,1)S(1)}, u32[]{:S(2)}, u32[]{:S(2)}) collective-permute-start(bf16[6,512]{1,0:T(8,128)(2,1)S(1)} %pad_maximum_fusion.1), channel_id=1, source_target_pairs={{0,8},{8,16},{16,24},{24,32},{32,40},{40,48},{48,56},{56,64},{64,7... | collective-permute-start | bytes 18440 | tf_op jit(solution)/shard_map/ppermute | solution.py:252
  6.7 5.1 %copy-start.3 = (f32[3,3,512]{2,1,0:T(4,128)S(1)}, f32[3,3,512]{2,1,0:T(4,128)}, u32[]{:S(2)}) copy-start(f32[3,3,512]{2,1,0:T(4,128)} %param.9) | copy-start | bytes 55300
  6.7 9.0 %all-to-all-start = ((f32[8,8,128]{2,1,0:T(8,128)}), f32[8,8,128]{2,1,0:T(8,128)S(1)}, u32[]{:S(2)}, u32[]{:S(2)}) async-start(f32[8,8,128]{2,1,0:T(8,128)} %broadcast_in_dim.12), calls=%async_computation | async-start | bytes 65536 | tf_op jit(solution)/shard_map/all_to_all | solution.py:256
  11.8 0.7 copy-start.5
  80.9 23.0 %copy-start.2 = (bf16[512,512]{1,0:T(8,128)(2,1)S(1)}, bf16[512,512]{1,0:T(8,128)(2,1)}, u32[]{:S(2)}) copy-start(bf16[512,512]{1,0:T(8,128)(2,1)} %query_ref.1) | copy-start | bytes 1572868

commit v2 on v1

v2 whole, which is shorter than its diff:
```python
import jax
import jax.numpy as jnp
from jax import lax
from jax.experimental import pallas as pl
from jax.experimental.pallas import tpu as pltpu
from jax.sharding import PartitionSpec as P

FILT = 8
TILE = 128
ROWS = 16
CHUNK = 72
GAIN = 16.0
SLOPE = 61.0
LIFT = 125.0
TINY = 1e-30
MIB = 1024 * 1024


def scale_of(peak):
    return jnp.maximum(peak, TINY).astype(jnp.bfloat16).astype(jnp.float32)


def encode(values, scale):
    level = jnp.log2(1.0 + jnp.abs(values) * (GAIN / scale))
    size = jnp.exp2(level * SLOPE - LIFT)
    return jnp.where(values < 0.0, -size, size)


def decode(codes, scale):
    level = (jnp.log2(jnp.abs(codes)) + LIFT) * (1.0 / SLOPE)
    size = (jnp.exp2(level) - 1.0) * (scale * (1.0 / GAIN))
    return jnp.where(codes < 0.0, -size, size)


def split(values):
    high = values.astype(jnp.bfloat16)
    low = (values - high.astype(jnp.float32)).astype(jnp.bfloat16)
    return high, low


def short_mix(stream, before, weights):
    length = stream.shape[1]
    lane = lax.broadcasted_iota(jnp.int32, stream.shape, 1)
    one = pltpu.roll(stream, 1, 1)
    one = jnp.where(lane == 0, before[:, 1:2], one)
    two = pltpu.roll(stream, 2, 1)
    two = jnp.where(lane == 0, before[:, 0:1], jnp.where(lane == 1, before[:, 1:2], two))
    return weights[0] * stream + weights[1] * one + weights[2] * two


def to_lanes(column):
    shape = (TILE, TILE)
    lane = lax.broadcasted_iota(jnp.int32, shape, 1)
    group = lax.broadcasted_iota(jnp.int32, shape, 0) // FILT
    spread = jnp.where(lane == group, column, 0.0)
    return spread.reshape(ROWS, FILT, TILE).sum(axis=0)


def edge_kernel(key_ref, value_ref, query_ref, out_ref, ends, arrived):
    length = key_ref.shape[1]
    copies = []
    for place, ref in enumerate((key_ref, value_ref, query_ref)):
        source = ref.at[:, pl.ds(length - TILE, TILE)]
        copies.append(pltpu.make_async_copy(source, ends.at[place], arrived.at[place]))
        copies[-1].start()
    row = lax.broadcasted_iota(jnp.int32, (8, TILE), 0)
    lane = lax.broadcasted_iota(jnp.int32, (8, TILE), 1)
    total = None
    for place, copy in enumerate(copies):
        copy.wait()
        pick = (row // 2 == place) & (lane == TILE - 2 + row % 2)
        part = lax.dot_general(
            pick.astype(jnp.bfloat16),
            ends[place],
            (((1,), (1,)), ((), ())),
            preferred_element_type=jnp.float32,
        )
        total = part if total is None else total + part
    out_ref[...] = total


def side_columns(weight_ref, skip_ref, rim_ref, cols):
    rows = [weight_ref[:, cols], skip_ref[:, cols], rim_ref[:6, cols]]
    return jnp.transpose(jnp.concatenate(rows, axis=0))


def product_of(key_ref, value_ref, side, rows):
    key = key_ref[rows, :].astype(jnp.float32)
    value = value_ref[rows, :].astype(jnp.float32)
    key_short = short_mix(key, side[:, 10:12], [side[:, n : n + 1] for n in range(3, 6)])
    value_short = short_mix(value, side[:, 12:14], [side[:, n : n + 1] for n in range(6, 9)])
    return key_short * value_short


def front_kernel(key_ref, value_ref, weight_ref, skip_ref, rim_ref, coded_ref, scale_ref):
    for step in range(key_ref.shape[0] // TILE):
        rows = slice(step * TILE, (step + 1) * TILE)
        side = side_columns(weight_ref, skip_ref, rim_ref, rows)
        product = product_of(key_ref, value_ref, side, rows)
        scale = scale_of(jnp.max(jnp.abs(product), axis=1, keepdims=True))
        coded_rows = encode(product, scale)
        for block in range(4):
            coded_ref[block, rows, :] = coded_rows[:, block * TILE : (block + 1) * TILE]
        scale_ref[step * FILT : (step + 1) * FILT, :] = to_lanes(scale)


def deal_kernel(coded_ref, scale_ref, taps_ref, out_ref):
    row = lax.broadcasted_iota(jnp.int32, (8, TILE), 0)
    tails = []
    for filt in range(FILT):
        taps = taps_ref[filt]
        tap_scale = scale_of(jnp.max(jnp.abs(taps)))
        tail = jnp.where(row == 5, tap_scale, 0.0)
        codes = encode(taps, tap_scale)
        for block in range(4):
            part = codes[:, block * TILE : (block + 1) * TILE]
            tail = jnp.where(row == block, part, tail)
        tails.append(tail)
    for dest in range(out_ref.shape[0]):
        step, filt = dest // FILT, dest % FILT
        for block in range(4):
            rows = pl.ds(step * TILE + filt, ROWS, stride=FILT)
            part = coded_ref[block, rows, :]
            out_ref[dest, block * ROWS : (block + 1) * ROWS, :] = part.astype(jnp.bfloat16)
        tail = jnp.where(row == 4, scale_ref[dest : dest + 1, :], tails[filt])
        out_ref[dest, 64:72, :] = tail.astype(jnp.bfloat16)


def gate_rows(streams, side, rows, local, query_out, base_out):
    query_ref, key_ref, value_ref = streams
    side = side[local, :]
    query = query_ref[rows, :].astype(jnp.float32)
    query_short = short_mix(query, side[:, 14:16], [side[:, n : n + 1] for n in range(3)])
    query_out[rows, :] = query_short
    product = product_of(key_ref, value_ref, side, rows)
    base_out[rows, :] = query_short * (side[:, 9:10] * product)


FINE = 512.0
GATE_FROM = 4


def unit_of(peak):
    power = jnp.exp2(7.0 - jnp.ceil(jnp.log2(jnp.maximum(peak, TINY))))
    return power.astype(jnp.bfloat16).astype(jnp.float32)


def four_parts(values):
    coarse = values.astype(jnp.bfloat16)
    wide = coarse.astype(jnp.float32)
    narrow = wide.astype(jnp.float8_e4m3fn)
    fine = ((values - wide) * FINE).astype(jnp.float8_e4m3fn)
    return coarse, narrow, fine


def conv_kernel(
    in_ref,
    query_ref,
    key_ref,
    value_ref,
    weight_ref,
    skip_ref,
    rim_ref,
    out_ref,
    query_out,
    base_out,
    main,
    cross,
    taps,
    toep,
    toep_narrow,
    toep_fine,
    total,
    back_unit,
):
    streams = (query_ref, key_ref, value_ref)
    count = in_ref.shape[0]
    blocks = count * 2
    size = blocks * ROWS
    lane = lax.broadcasted_iota(jnp.int32, (ROWS, TILE), 1)
    row = lax.broadcasted_iota(jnp.int32, (ROWS, TILE), 0)
    diagonal = lane == row
    pick = lax.broadcasted_iota(jnp.int32, (8, TILE), 0) == 0
    wide_lane = lax.broadcasted_iota(jnp.int32, (TILE, TILE), 1)
    causal = wide_lane >= lax.broadcasted_iota(jnp.int32, (TILE, TILE), 0)

    def tail_of(src):
        return in_ref[src, pl.ds(64, 8), :].astype(jnp.float32)

    peaks = tail_of(0)
    for src in range(1, count):
        peaks = jnp.maximum(peaks, tail_of(src))
    unit = unit_of(jnp.sum(jnp.where(diagonal, peaks[4:5, :], 0.0), axis=1, keepdims=True))
    tap_unit = unit_of(peaks[5:6, 0:1])
    back_unit[...] = jnp.broadcast_to(1.0 / (unit * tap_unit), (ROWS, TILE))

    def unpack(src, carry):
        tail = tail_of(src)
        scale = jnp.sum(jnp.where(diagonal, tail[4:5, :], 0.0), axis=1, keepdims=True) * unit
        taps[pl.ds(src * 4, 4), :] = decode(tail[0:4, :], tail[5:6, :] * tap_unit)
        at = pl.ds(pl.multiple_of(src * 32, 32), 32)
        for half in range(2):
            pair = []
            for block in (half, half + 2):
                part = in_ref[src, pl.ds(block * ROWS, ROWS), :].astype(jnp.float32)
                pair.append(decode(part, scale))
            coarse, narrow, fine = four_parts(jnp.concatenate(pair, axis=0))
            main[at, pl.ds(half * TILE, TILE)] = coarse
            cross[at, pl.ds(half * TILE, TILE)] = fine
            cross[at, pl.ds((half + 2) * TILE, TILE)] = narrow
        return carry

    def build(tile, before):
        line = jnp.broadcast_to(taps[tile : tile + 1, :], (TILE, TILE))
        rolled = pltpu.roll(line, 0, 1, stride=1, stride_axis=0)
        coarse, narrow, fine = four_parts(jnp.where(causal, rolled, before))
        toep[tile + 1] = coarse
        toep_narrow[tile + 1] = narrow
        toep_fine[tile + 1] = fine
        return rolled

    def weight(ref, lag):
        top = jnp.concatenate([ref[2 * lag + 1], ref[2 * lag + 2]], axis=1)
        bottom = jnp.concatenate([ref[2 * lag], ref[2 * lag + 1]], axis=1)
        return jnp.concatenate([top, bottom], axis=0)

    def pack(dst):
        parts = []
        for block in range(4):
            at = pl.ds(dst * 32 + (block // 2) * ROWS, ROWS)
            parts.append(total[at, pl.ds((block % 2) * TILE, TILE)])
        peak = jnp.maximum(
            jnp.maximum(jnp.abs(parts[0]), jnp.abs(parts[1])),
            jnp.maximum(jnp.abs(parts[2]), jnp.abs(parts[3])),
        )
        scale = scale_of(jnp.max(peak, axis=1, keepdims=True))
        for block in range(4):
            codes = encode(parts[block], scale).astype(jnp.bfloat16)
            out_ref[dst, pl.ds(block * ROWS, ROWS), :] = codes
        sent = jnp.where(diagonal, scale * back_unit[...], 0.0)
        spread = jnp.sum(sent, axis=0, keepdims=True)
        out_ref[dst, pl.ds(64, 8), :] = jnp.where(pick, spread, 0.0).astype(jnp.bfloat16)

    lax.fori_loop(0, count, unpack, 0, unroll=8)
    toep[0] = jnp.zeros((TILE, TILE), toep.dtype)
    toep_narrow[0] = jnp.zeros((TILE, TILE), toep_narrow.dtype)
    toep_fine[0] = jnp.zeros((TILE, TILE), toep_fine.dtype)
    rolled = build(1, build(0, jnp.zeros((TILE, TILE), jnp.float32)))
    for lag in range(blocks):
        if lag + 1 < blocks:
            rolled = build(2 * lag + 3, build(2 * lag + 2, rolled))
        rows = size - lag * ROWS
        part = jnp.dot(main[:rows, :], weight(toep, lag), preferred_element_type=jnp.float32)
        narrow = jnp.concatenate([weight(toep_narrow, lag), weight(toep_fine, lag)], axis=0)
        rest = jnp.dot(cross[:rows, :], narrow, preferred_element_type=jnp.float32)
        part = part + rest * (1.0 / FINE)
        if lag == 0:
            total[...] = part
        else:
            total[lag * ROWS :, :] += part
        if lag % 2 == 1:
            pack(lag // 2)
        if GATE_FROM <= lag < GATE_FROM + 3 * 16 and (lag - GATE_FROM) % 3 == 0:
            piece = (lag - GATE_FROM) // 3
            if piece % 4 == 0:
                cols = slice(piece * 32, piece * 32 + TILE)
                side = side_columns(weight_ref, skip_ref, rim_ref, cols)
            rows = slice(piece * 32, (piece + 1) * 32)
            local_rows = slice(piece % 4 * 32, piece % 4 * 32 + 32)
            gate_rows(streams, side, rows, local_rows, query_out, base_out)


def conv(chunks, streams, weight, skip, rim):
    count = chunks.shape[0]
    plane = jax.ShapeDtypeStruct(streams[0].shape, jnp.float32)
    size = count * 2 * ROWS
    tiles = (count * 4 + 1, TILE, TILE)
    whole = pl.BlockSpec(memory_space=pltpu.VMEM)
    return pl.pallas_call(
        conv_kernel,
        in_specs=[whole] * 7,
        out_specs=[whole] * 3,
        out_shape=[jax.ShapeDtypeStruct(chunks.shape, jnp.bfloat16), plane, plane],
        scratch_shapes=[
            pltpu.VMEM((size, 2 * TILE), jnp.bfloat16),
            pltpu.VMEM((size, 4 * TILE), jnp.float8_e4m3fn),
            pltpu.VMEM((count * 4, TILE), jnp.float32),
            pltpu.VMEM(tiles, jnp.bfloat16),
            pltpu.VMEM(tiles, jnp.float8_e4m3fn),
            pltpu.VMEM(tiles, jnp.float8_e4m3fn),
            pltpu.VMEM((size, 2 * TILE), jnp.float32),
            pltpu.VMEM((ROWS, TILE), jnp.float32),
        ],
        compiler_params=pltpu.CompilerParams(vmem_limit_bytes=24 * MIB),
        name="conv",
    )(chunks, *streams, weight, skip, rim)


def back_kernel(in_ref, query_ref, base_ref, out_ref, plain):
    lane = lax.broadcasted_iota(jnp.int32, (ROWS, TILE), 1)
    row = lax.broadcasted_iota(jnp.int32, (ROWS, TILE), 0)
    step = pl.program_id(0)
    for filt in range(FILT):
        src = step * FILT + filt
        tail = in_ref[src, pl.ds(64, 8), :].astype(jnp.float32)
        scale = jnp.sum(jnp.where(lane == row, tail[0:1, :], 0.0), axis=1, keepdims=True)
        for block in range(4):
            part = in_ref[src, pl.ds(block * ROWS, ROWS), :].astype(jnp.float32)
            plain[block, pl.ds(filt, ROWS, stride=FILT), :] = decode(part, scale)
    rows = pl.ds(pl.multiple_of(step * TILE, TILE), TILE)
    long = jnp.concatenate([plain[block] for block in range(4)], axis=1)
    out_ref[...] = (query_ref[rows, :] * long + base_ref[rows, :]).astype(jnp.bfloat16)


WHOLE = pl.BlockSpec(memory_space=pltpu.VMEM)


def whole_call(kernel, name, outs, *operands):
    return pl.pallas_call(
        kernel,
        in_specs=[WHOLE] * len(operands),
        out_specs=[WHOLE] * len(outs),
        out_shape=[jax.ShapeDtypeStruct(shape, dtype) for shape, dtype in outs],
        compiler_params=pltpu.CompilerParams(vmem_limit_bytes=16 * MIB),
        name=name,
    )(*operands)


def edge(key_proj, value_proj, query_proj):
    rows = key_proj.shape[0]
    return pl.pallas_call(
        edge_kernel,
        in_specs=[pl.BlockSpec(memory_space=pl.ANY)] * 3,
        out_specs=WHOLE,
        out_shape=jax.ShapeDtypeStruct((8, rows), jnp.float32),
        scratch_shapes=[
            pltpu.VMEM((3, rows, TILE), key_proj.dtype),
            pltpu.SemaphoreType.DMA((3,)),
        ],
        name="edge",
    )(key_proj, value_proj, query_proj)


def back(chunks, query_short, base):
    rows, length = base.shape
    return pl.pallas_call(
        back_kernel,
        grid=(rows // TILE,),
        in_specs=[WHOLE] * 3,
        out_specs=pl.BlockSpec((TILE, length), lambda n: (n, 0)),
        out_shape=jax.ShapeDtypeStruct((rows, length), jnp.bfloat16),
        scratch_shapes=[pltpu.VMEM((4, TILE, TILE), jnp.float32)],
        compiler_params=pltpu.CompilerParams(vmem_limit_bytes=16 * MIB),
        name="back",
    )(chunks, query_short, base)


def local(query_proj, key_proj, value_proj, short_weight, skip_bias, filter_taps):
    count = lax.axis_size("context")
    rows, length = query_proj.shape
    taps = jnp.broadcast_to(filter_taps[:, None, :], (FILT, 1, length))
    taps = lax.all_to_all(taps, "tensor", 0, 0, tiled=True)
    rim = edge(key_proj, value_proj, query_proj)
    rim = lax.ppermute(rim, "context", [(n, n + 1) for n in range(count - 1)])
    weight = short_weight.reshape(9, rows)
    skip = skip_bias[None, :]
    outs = [((4, rows, TILE), jnp.float32), ((count, TILE), jnp.float32)]
    coded, scales = whole_call(
        front_kernel, "front", outs, key_proj, value_proj, weight, skip, rim
    )
    outs = [((count, CHUNK, TILE), jnp.bfloat16)]
    (chunks,) = whole_call(deal_kernel, "deal", outs, coded, scales, taps)
    chunks = lax.all_to_all(chunks, "context", 0, 0, tiled=True)
    streams = (query_proj, key_proj, value_proj)
    chunks, query_short, base = conv(chunks, streams, weight, skip, rim)
    chunks = lax.all_to_all(chunks, "context", 0, 0, tiled=True)
    return back(chunks, query_short, base)


def solution(mesh):
    in_specs = (
        P("tensor", "context"),
        P("tensor", "context"),
        P("tensor", "context"),
        P(None, None, "tensor"),
        P("tensor"),
        P("tensor", "context"),
    )
    out_specs = P("tensor", "context")
    return jax.shard_map(local, mesh=mesh, in_specs=in_specs, out_specs=out_specs, check_vma=False)
```

time: 107 us -> 82.9 us (0.77)
  Pallas kernels: 37.9 us -> 19 us
  local copies, waits for them, and re-layouts: 3.9 us -> 1.29 us
  waiting for transfers between devices: 3.27 us -> 0.8 us
    pallas_call x3 -> x5, Pallas kernels: 37.9 us -> 19 us  [the longest x1 12 us: conv(): pl.pallas_call(conv_kernel, in_specs=[whole] * 7, out_specs=[whole] * 3,...]
    all_to_all x1, waiting for transfers between devices: 3.26 us -> 0.8 us  [local(): taps = lax.all_to_all(taps, 'tensor', 0, 0, tiled=True)]
    slice x3 -> x0, local copies, waits for them, and re-layouts: 2.26 us -> none  [local(): stream[:, -2:]]
  transfers between devices with their start and end apart: 2 -> 2, of which waited for: 1 -> 1; matrix products, arithmetic and copies ran while one was open for 1% -> 1% of each run, Pallas kernels for 0% -> 3%
where the time goes in v2:
time: 82.9 us; the launch traced here: 82.2 us
  blocking collectives  52.8 us (64%)
  Pallas kernels  19 us (23%)
  starting transfers between devices  8.31 us (10%)
  local copies, waits for them, and re-layouts  1.29 us (2%)
    all_to_all x2, blocking collectives, local(): chunks = lax.all_to_all(chunks, 'context', 0, 0, tiled=True)  52.8 us
    pallas_call x1, Pallas kernels, conv(): pl.pallas_call(conv_kernel, in_specs=[whole] * 7, out_specs=[whole] * 3,...  12 us
    all_to_all x1, starting transfers between devices, local(): taps = lax.all_to_all(taps, 'tensor', 0, 0, tiled=True)  4.92 us
    ppermute x1, starting transfers between devices, local(): rim = lax.ppermute(rim, 'context', [(n, n + 1) for n in range(count - 1)])  3.4 us
    pallas_call x2, Pallas kernels, whole_call(): pl.pallas_call(kernel, in_specs=[WHOLE] * len(operands), out_specs=[WHOLE...  3.06 us
    pallas_call x1, Pallas kernels, back(): pl.pallas_call(back_kernel, grid=(rows // TILE,), in_specs=[WHOLE] * 3, o...  1.93 us
    pallas_call x1, Pallas kernels, edge(): pl.pallas_call(edge_kernel, in_specs=[pl.BlockSpec(memory_space=pl.ANY)]...  1.92 us
  transfers between devices with their start and end apart: 2, of which 1 were waited for; matrix products, arithmetic and copies ran while one was open for 1% of the time, Pallas kernels for 3%

profile of v2, /device:TPU:8, one launch (start us, length us, event | category | flops | bytes accessed | tf_op | source)
XLA Modules:
  0.0 82.2 jit_solution(9697582776166362686)
XLA Ops:
  0.0 0.0 copy-start.1
  0.0 0.0 copy-start
  0.0 0.0 copy-start.5
  0.0 1.9 %edge.1 = f32[8,512]{1,0:T(8,128)} custom-call(bf16[512,512]{1,0:T(8,128)(2,1)} %key_ref.5, bf16[512,512]{1,0:T(8,128)(2,1)} %value_ref.5, bf16[512,512]{1,0:T(8,128)(2,1)} %query_ref.3), custom_call_target="tpu_custom_call" | custom-call | tf_op jit(solution)/shard_map/edge/pallas_call | solution.py:331
  1.9 3.4 %collective-permute-start = (f32[8,512]{1,0:T(8,128)}, f32[8,512]{1,0:T(8,128)S(1)}, u32[]{:S(2)}, u32[]{:S(2)}) collective-permute-start(f32[8,512]{1,0:T(8,128)} %edge.1), channel_id=1, source_target_pairs={{0,8},{8,16},{16,24},{24,32},{32,40},{40,48},{48,56},{56,64},{64,7... | collective-permute-start | bytes 49160 | tf_op jit(solution)/shard_map/ppermute | solution.py:364
  5.3 0.0 copy-done.5
  5.3 0.0 copy-start.4
  5.4 0.6 broadcast_in_dim.13
  6.0 4.9 %all-to-all-start = ((f32[8,1,512]{2,1,0:T(1,128)}), f32[8,1,512]{2,1,0:T(1,128)S(1)}, u32[]{:S(2)}, u32[]{:S(2)}) async-start(f32[8,1,512]{2,1,0:T(1,128)} %broadcast_in_dim.13), calls=%async_computation | async-start | bytes 32768 | tf_op jit(solution)/shard_map/all_to_all | solution.py:362
  10.9 0.0 copy-done.4
  10.9 0.0 copy-start.3
  10.9 0.0 collective-permute-done.rim_ref
  10.9 0.0 copy-done.1
  10.9 0.0 copy-done
  10.9 0.6 copy-done.3
  11.6 2.4 %front.1 = (f32[4,512,128]{2,1,0:T(8,128)S(1)}, f32[32,128]{1,0:T(8,128)S(1)}) custom-call(bf16[512,512]{1,0:T(8,128)(2,1)S(1)} %copy-done, bf16[512,512]{1,0:T(8,128)(2,1)S(1)} %copy-done.1, f32[9,512]{1,0:T(8,128)S(1)} %reshape.6.weight_ref, f32[1,512]{1,0:T(1,128)S(1)} %bitcast.2, f32[8,512]{1,0:T(8,128)S(1)} %collective-permute-done.rim_ref), custom_call_target="tpu_custom_call" | custom-call | tf_op jit(solution)/shard_map/front/pallas_call | solution.py:319
  14.0 0.8 all-to-all-done.taps_ref
  14.8 0.7 deal.1
  15.5 0.0 copy-start.2
  15.5 29.9 %all_to_all.15.in_ref = bf16[32,72,128]{2,1,0:T(8,128)(2,1)S(1)} all-to-all(bf16[32,72,128]{2,1,0:T(8,128)(2,1)S(1)} %deal.1), channel_id=1, replica_groups=mesh['context'=32,'tensor'=8] {'context'}, dimensions={0} | all-to-all | bytes 1179648 | tf_op jit(solution)/shard_map/all_to_all | solution.py:373
  45.4 0.0 copy-done.2
  45.4 12.0 %conv.1 = (bf16[32,72,128]{2,1,0:T(8,128)(2,1)S(1)}, f32[512,512]{1,0:T(8,128)S(1)}, f32[512,512]{1,0:T(8,128)S(1)}) custom-call(bf16[32,72,128]{2,1,0:T(8,128)(2,1)S(1)} %all_to_all.15.in_ref, bf16[512,512]{1,0:T(8,128)(2,1)S(1)} %copy-done.2, bf16[512,512]{1,0:T(8,128)(2,1)S(1)} %copy-done, bf16[512,512]{1,0:T(8,128)(2,1)S(1)} %copy-done.1, ...), custom_call_target="tpu_custom_call" | custom-call | tf_op jit(solution)/shard_map/conv/pallas_call | solution.py:279
  57.4 22.9 %all_to_all.16.in_ref = bf16[32,72,128]{2,1,0:T(8,128)(2,1)S(1)} all-to-all(bf16[32,72,128]{2,1,0:T(8,128)(2,1)S(1)} %get-tuple-element.12), channel_id=1, replica_groups=mesh['context'=32,'tensor'=8] {'context'}, dimensions={0} | all-to-all | bytes 1179648 | tf_op jit(solution)/shard_map/all_to_all | solution.py:376
  80.3 1.9 %back.1 = bf16[512,512]{1,0:T(8,128)(2,1)} custom-call(bf16[32,72,128]{2,1,0:T(8,128)(2,1)S(1)} %all_to_all.16.in_ref, f32[512,512]{1,0:T(8,128)S(1)} %get-tuple-element.13.query_ref, f32[512,512]{1,0:T(8,128)S(1)} %get-tuple-element.14.base_ref), custom_call_target="tpu_custom_call" | custom-call | tf_op jit(solution)/shard_map/back/pallas_call | solution.py:346
  (1 shorter events, 0.0 us)
Async XLA Ops:
  0.0 10.9 %copy-start.1 = (bf16[512,512]{1,0:T(8,128)(2,1)S(1)}, bf16[512,512]{1,0:T(8,128)(2,1)}, u32[]{:S(2)}) copy-start(bf16[512,512]{1,0:T(8,128)(2,1)} %value_ref.5) | copy-start | bytes 1572868
  0.0 10.9 %copy-start = (bf16[512,512]{1,0:T(8,128)(2,1)S(1)}, bf16[512,512]{1,0:T(8,128)(2,1)}, u32[]{:S(2)}) copy-start(bf16[512,512]{1,0:T(8,128)(2,1)} %key_ref.5) | copy-start | bytes 1572868
  0.0 5.3 %copy-start.5 = (f32[1,512]{1,0:T(1,128)S(1)}, f32[1,512]{1,0:T(1,128)}, u32[]{:S(2)}) copy-start(f32[1,512]{1,0:T(1,128)} %param.11) | copy-start | bytes 6148
  1.9 9.0 %collective-permute-start = (f32[8,512]{1,0:T(8,128)}, f32[8,512]{1,0:T(8,128)S(1)}, u32[]{:S(2)}, u32[]{:S(2)}) collective-permute-start(f32[8,512]{1,0:T(8,128)} %edge.1), channel_id=1, source_target_pairs={{0,8},{8,16},{16,24},{24,32},{32,40},{40,48},{48,56},{56,64},{64,7... | collective-permute-start | bytes 49160 | tf_op jit(solution)/shard_map/ppermute | solution.py:364
  5.3 5.5 %copy-start.4 = (f32[3,3,512]{2,1,0:T(4,128)S(1)}, f32[3,3,512]{2,1,0:T(4,128)}, u32[]{:S(2)}) copy-start(f32[3,3,512]{2,1,0:T(4,128)} %param.9) | copy-start | bytes 55300
  6.0 8.8 %all-to-all-start = ((f32[8,1,512]{2,1,0:T(1,128)}), f32[8,1,512]{2,1,0:T(1,128)S(1)}, u32[]{:S(2)}, u32[]{:S(2)}) async-start(f32[8,1,512]{2,1,0:T(1,128)} %broadcast_in_dim.13), calls=%async_computation | async-start | bytes 32768 | tf_op jit(solution)/shard_map/all_to_all | solution.py:362
  10.9 0.7 copy-start.3
  15.5 29.9 %copy-start.2 = (bf16[512,512]{1,0:T(8,128)(2,1)S(1)}, bf16[512,512]{1,0:T(8,128)(2,1)}, u32[]{:S(2)}) copy-start(bf16[512,512]{1,0:T(8,128)(2,1)} %query_ref.3) | copy-start | bytes 1572868

commit v3 on v2

v3 whole, which is shorter than its diff:
```python
import jax
import jax.numpy as jnp
from jax import lax
from jax.experimental import pallas as pl
from jax.experimental.pallas import tpu as pltpu
from jax.sharding import PartitionSpec as P

FILT = 8
TILE = 128
ROWS = 16
CHUNK = 72
GAIN = 16.0
SLOPE = 61.0
LIFT = 125.0
TINY = 1e-30
MIB = 1024 * 1024


def scale_of(peak):
    return jnp.maximum(peak, TINY).astype(jnp.bfloat16).astype(jnp.float32)


def encode(values, scale):
    level = jnp.log2(1.0 + jnp.abs(values) * (GAIN / scale))
    size = jnp.exp2(level * SLOPE - LIFT)
    return jnp.where(values < 0.0, -size, size)


def decode(codes, scale):
    level = (jnp.log2(jnp.abs(codes)) + LIFT) * (1.0 / SLOPE)
    size = (jnp.exp2(level) - 1.0) * (scale * (1.0 / GAIN))
    return jnp.where(codes < 0.0, -size, size)


def split(values):
    high = values.astype(jnp.bfloat16)
    low = (values - high.astype(jnp.float32)).astype(jnp.bfloat16)
    return high, low


def short_mix(stream, weights):
    one = pltpu.roll(stream, 1, 1)
    two = pltpu.roll(stream, 2, 1)
    return weights[0] * stream + weights[1] * one + weights[2] * two


def to_lanes(column):
    shape = (TILE, TILE)
    lane = lax.broadcasted_iota(jnp.int32, shape, 1)
    group = lax.broadcasted_iota(jnp.int32, shape, 0) // FILT
    spread = jnp.where(lane == group, column, 0.0)
    return spread.reshape(ROWS, FILT, TILE).sum(axis=0)


def side_columns(rows):
    missing = 16 - sum(part.shape[0] for part in rows)
    rows = rows + [jnp.zeros((missing, TILE), jnp.float32)]
    return jnp.transpose(jnp.concatenate(rows, axis=0))


def product_of(key_ref, value_ref, side, rows):
    key = key_ref[rows, :].astype(jnp.float32)
    value = value_ref[rows, :].astype(jnp.float32)
    key_short = short_mix(key, [side[:, n : n + 1] for n in range(3, 6)])
    value_short = short_mix(value, [side[:, n : n + 1] for n in range(6, 9)])
    return key_short * value_short


def ends_of(refs, start):
    shape = (TILE, TILE)
    lane = lax.broadcasted_iota(jnp.int32, shape, 1)
    place = lax.broadcasted_iota(jnp.int32, shape, 0)
    total = None
    for index, ref in enumerate(refs):
        pick = (lane // 32 == index) & (place == start % TILE + lane % 32 // 16)
        part = jnp.dot(
            ref[:, start // TILE * TILE : start // TILE * TILE + TILE],
            pick.astype(jnp.bfloat16),
            preferred_element_type=jnp.float32,
        )
        total = part if total is None else total + part
    return total


def front_kernel(key_ref, value_ref, query_ref, weight_ref, coded_ref, scale_ref, ends_ref):
    length = key_ref.shape[1]
    refs = (key_ref, value_ref, query_ref)
    group = lax.broadcasted_iota(jnp.int32, (TILE, TILE), 0) // FILT
    own = lax.broadcasted_iota(jnp.int32, (TILE, TILE), 1) % ROWS == group
    lane = lax.broadcasted_iota(jnp.int32, (TILE, length), 1)
    both = [ends_of(refs, 0), ends_of(refs, length - 2)]
    for step in range(key_ref.shape[0] // TILE):
        rows = slice(step * TILE, (step + 1) * TILE)
        dests = slice(step * FILT, (step + 1) * FILT)
        for which in range(2):
            spread = jnp.where(own, both[which][rows, :], 0.0)
            ends_ref[which, dests, :] = spread.reshape(ROWS, FILT, TILE).sum(axis=0)
        side = side_columns([weight_ref[:, rows]])
        product = jnp.where(lane < 2, 0.0, product_of(key_ref, value_ref, side, rows))
        scale = scale_of(jnp.max(jnp.abs(product), axis=1, keepdims=True))
        coded_rows = encode(product, scale)
        for block in range(4):
            coded_ref[block, rows, :] = coded_rows[:, block * TILE : (block + 1) * TILE]
        scale_ref[dests, :] = to_lanes(scale)


def deal_kernel(coded_ref, scale_ref, ends_ref, taps_ref, out_ref):
    row = lax.broadcasted_iota(jnp.int32, (8, TILE), 0)
    tails = []
    for filt in range(FILT):
        taps = taps_ref[filt]
        tap_scale = scale_of(jnp.max(jnp.abs(taps)))
        tail = jnp.where(row == 5, tap_scale, 0.0)
        codes = encode(taps, tap_scale)
        for block in range(4):
            part = codes[:, block * TILE : (block + 1) * TILE]
            tail = jnp.where(row == block, part, tail)
        tails.append(tail)
    for dest in range(out_ref.shape[0]):
        step, filt = dest // FILT, dest % FILT
        for block in range(4):
            rows = pl.ds(step * TILE + filt, ROWS, stride=FILT)
            part = coded_ref[block, rows, :]
            out_ref[dest, block * ROWS : (block + 1) * ROWS, :] = part.astype(jnp.bfloat16)
        tail = jnp.where(row == 4, scale_ref[dest : dest + 1, :], tails[filt])
        tail = jnp.where(row == 6, ends_ref[0, dest : dest + 1, :], tail)
        tail = jnp.where(row == 7, ends_ref[1, dest : dest + 1, :], tail)
        out_ref[dest, 64:72, :] = tail.astype(jnp.bfloat16)


def gate_rows(streams, side, rows, local, query_out, base_out):
    query_ref, key_ref, value_ref = streams
    side = side[local, :]
    query = query_ref[rows, :].astype(jnp.float32)
    query_short = short_mix(query, [side[:, n : n + 1] for n in range(3)])
    query_out[rows, :] = query_short
    product = product_of(key_ref, value_ref, side, rows)
    base_out[rows, :] = query_short * (side[:, 9:10] * product)


FINE = 512.0
GATE_FROM = 2
GATE_STEP = 2
EARLY = 12
PER_STEP = 3


def unit_of(peak):
    power = jnp.exp2(7.0 - jnp.ceil(jnp.log2(jnp.maximum(peak, TINY))))
    return power.astype(jnp.bfloat16).astype(jnp.float32)


def four_parts(values):
    coarse = values.astype(jnp.bfloat16)
    wide = coarse.astype(jnp.float32)
    narrow = wide.astype(jnp.float8_e4m3fn)
    fine = ((values - wide) * FINE).astype(jnp.float8_e4m3fn)
    return coarse, narrow, fine


def own_weights(weight_ref, skip_ref):
    index = lax.axis_index("context")
    cols = pl.ds(pl.multiple_of(index // FILT * TILE, TILE), TILE)
    source = lax.broadcasted_iota(jnp.int32, (TILE, TILE), 0)
    lane = lax.broadcasted_iota(jnp.int32, (TILE, TILE), 1)
    pick = (source % FILT == index % FILT) & (source // FILT == lane % ROWS)
    zeros = jnp.zeros((6, TILE), jnp.float32)
    rows = jnp.concatenate([weight_ref[:, cols], skip_ref[:, cols], zeros], axis=0)
    return jnp.dot(
        rows,
        pick.astype(jnp.float32),
        precision=lax.Precision.HIGHEST,
        preferred_element_type=jnp.float32,
    )


def start_mix(first, before, weights):
    lane = lax.broadcasted_iota(jnp.int32, first.shape, 1)
    taps = []
    for lag in range(3):
        query, key, value = [weights[3 * n + lag : 3 * n + lag + 1, :] for n in range(3)]
        taps.append(jnp.where(lane < 32, key, jnp.where(lane < 64, value, query)))
    second = lane % 32 >= ROWS
    one = jnp.where(second, pltpu.roll(first, ROWS, 1), pltpu.roll(before, TILE - ROWS, 1))
    return taps[0] * first + taps[1] * one + taps[2] * before, weights[9:10, :]


def conv_kernel(
    in_ref,
    query_ref,
    key_ref,
    value_ref,
    weight_ref,
    skip_ref,
    out_ref,
    query_out,
    base_out,
    main,
    cross,
    taps,
    toep,
    toep_narrow,
    toep_fine,
    total,
    back_unit,
    first,
    last,
    start_prod,
    start_gate,
    start_base,
):
    streams = (query_ref, key_ref, value_ref)
    count = in_ref.shape[0]
    blocks = count * 2
    size = blocks * ROWS
    lane = lax.broadcasted_iota(jnp.int32, (ROWS, TILE), 1)
    row = lax.broadcasted_iota(jnp.int32, (ROWS, TILE), 0)
    diagonal = lane == row
    beside = lane == row + ROWS
    tail_row = lax.broadcasted_iota(jnp.int32, (8, TILE), 0)
    wide_lane = lax.broadcasted_iota(jnp.int32, (TILE, TILE), 1)
    causal = wide_lane >= lax.broadcasted_iota(jnp.int32, (TILE, TILE), 0)

    def tail_of(src):
        return in_ref[src, pl.ds(64, 8), :].astype(jnp.float32)

    last[0:1, :] = jnp.zeros((1, TILE), jnp.float32)
    peaks = None
    for src in range(count):
        tail = tail_of(src)
        peaks = tail if peaks is None else jnp.maximum(peaks, tail)
        taps[src * 4 : (src + 1) * 4, :] = decode(tail[0:4, :], tail[5:6, :])
        first[src : src + 1, :] = tail[6:7, :]
        last[src + 1 : src + 2, :] = tail[7:8, :]
    lane_weights = own_weights(weight_ref, skip_ref)
    mixed, skip = start_mix(first[...], last[0:count, :], lane_weights)
    product = mixed * pltpu.roll(mixed, TILE - 32, 1)
    query = pltpu.roll(mixed, TILE - 64, 1)
    start_prod[...] = product
    start_gate[...] = query
    start_base[...] = query * (skip * product)

    def column(mask, line):
        return jnp.sum(jnp.where(mask, line, 0.0), axis=1, keepdims=True)

    start_peak = jnp.max(jnp.abs(product), axis=0, keepdims=True)
    start_peak = jnp.maximum(column(diagonal, start_peak), column(beside, start_peak))
    unit = unit_of(jnp.maximum(column(diagonal, peaks[4:5, :]), start_peak))
    tap_unit = unit_of(peaks[5:6, 0:1])
    back_unit[...] = jnp.broadcast_to(1.0 / (unit * tap_unit), (ROWS, TILE))

    def unpack(src):
        tail = tail_of(src)
        scale = column(diagonal, tail[4:5, :]) * unit
        starts = start_prod[src : src + 1, :]
        early = jnp.where(lane == 0, column(diagonal, starts), column(beside, starts)) * unit
        at = slice(src * 32, (src + 1) * 32)
        for half in range(2):
            pair = []
            for block in (half, half + 2):
                part = in_ref[src, pl.ds(block * ROWS, ROWS), :].astype(jnp.float32)
                values = decode(part, scale)
                pair.append(jnp.where(lane < 2, early, values) if block == 0 else values)
            coarse, narrow, fine = four_parts(jnp.concatenate(pair, axis=0))
            main[at, pl.ds(half * TILE, TILE)] = coarse
            cross[at, pl.ds(half * TILE, TILE)] = fine
            cross[at, pl.ds((half + 2) * TILE, TILE)] = narrow

    def rolled(tile):
        line = jnp.broadcast_to(taps[tile : tile + 1, :] * tap_unit, (TILE, TILE))
        return pltpu.roll(line, 0, 1, stride=1, stride_axis=0)

    def build(tile, before):
        here = rolled(tile)
        coarse, narrow, fine = four_parts(jnp.where(causal, here, before))
        toep[tile + 1] = coarse
        toep_narrow[tile + 1] = narrow
        toep_fine[tile + 1] = fine
        return here

    def weight(ref, lag):
        top = jnp.concatenate([ref[2 * lag + 1], ref[2 * lag + 2]], axis=1)
        bottom = jnp.concatenate([ref[2 * lag], ref[2 * lag + 1]], axis=1)
        return jnp.concatenate([top, bottom], axis=0)

    def pack(dst):
        parts = []
        for block in range(4):
            at = pl.ds(dst * 32 + (block // 2) * ROWS, ROWS)
            parts.append(total[at, pl.ds((block % 2) * TILE, TILE)])
        peak = jnp.maximum(
            jnp.maximum(jnp.abs(parts[0]), jnp.abs(parts[1])),
            jnp.maximum(jnp.abs(parts[2]), jnp.abs(parts[3])),
        )
        scale = scale_of(jnp.max(peak, axis=1, keepdims=True))
        for block in range(4):
            codes = encode(parts[block], scale).astype(jnp.bfloat16)
            out_ref[dst, pl.ds(block * ROWS, ROWS), :] = codes
        sent = jnp.where(diagonal, scale * back_unit[...], 0.0)
        spread = jnp.sum(sent, axis=0, keepdims=True)
        plain = parts[0] * back_unit[...]
        long = jnp.where(diagonal, plain[:, 0:1], jnp.where(beside, plain[:, 1:2], 0.0))
        long = jnp.sum(long, axis=0, keepdims=True)
        ends = start_gate[dst : dst + 1, :] * long + start_base[dst : dst + 1, :]
        tail = jnp.where(tail_row == 0, spread, jnp.where(tail_row == 1, ends, 0.0))
        out_ref[dst, pl.ds(64, 8), :] = tail.astype(jnp.bfloat16)

    def lag_step(lag):
        rows = size - lag * ROWS
        part = jnp.dot(main[:rows, :], weight(toep, lag), preferred_element_type=jnp.float32)
        narrow = jnp.concatenate([weight(toep_narrow, lag), weight(toep_fine, lag)], axis=0)
        rest = jnp.dot(cross[:rows, :], narrow, preferred_element_type=jnp.float32)
        total[lag * ROWS :, :] += part + rest * (1.0 / FINE)

    def gate(piece, side):
        rows = slice(piece * 32, (piece + 1) * 32)
        local_rows = slice(piece % 4 * 32, piece % 4 * 32 + 32)
        gate_rows(streams, side, rows, local_rows, query_out, base_out)

    total[...] = jnp.zeros_like(total)
    toep[0] = jnp.zeros((TILE, TILE), toep.dtype)
    toep_narrow[0] = jnp.zeros((TILE, TILE), toep_narrow.dtype)
    toep_fine[0] = jnp.zeros((TILE, TILE), toep_fine.dtype)
    early = blocks * EARLY // 64
    ready = early // 2
    for src in range(ready):
        unpack(src)
    order = list(range(blocks - early, blocks)) + list(range(blocks - early))
    built = rolled(2 * order[0] - 1)
    built = build(2 * order[0] + 1, build(2 * order[0], build(2 * order[0] - 1, rolled(2 * order[0] - 2))))
    for index, lag in enumerate(order):
        if index + 1 < blocks:
            ahead = order[index + 1]
            if ahead == 0:
                built = jnp.zeros((TILE, TILE), jnp.float32)
            built = build(2 * ahead + 1, build(2 * ahead, built))
        lag_step(lag)
        while ready < min(count, early // 2 + (index + 1) * PER_STEP):
            unpack(ready)
            ready += 1
        place = index - early
        if place >= 0 and lag % 2 == 1:
            pack(lag // 2)
        if place >= GATE_FROM and (place - GATE_FROM) % GATE_STEP == 0:
            piece = (place - GATE_FROM) // GATE_STEP
            if piece < 16:
                if piece % 4 == 0:
                    cols = slice(piece * 32, piece * 32 + TILE)
                    side = side_columns([weight_ref[:, cols], skip_ref[:, cols]])
                gate(piece, side)
    for dst in range((blocks - early) // 2, count):
        pack(dst)


def conv(chunks, streams, weight, skip):
    count = chunks.shape[0]
    plane = jax.ShapeDtypeStruct(streams[0].shape, jnp.float32)
    size = count * 2 * ROWS
    tiles = (count * 4 + 1, TILE, TILE)
    whole = pl.BlockSpec(memory_space=pltpu.VMEM)
    return pl.pallas_call(
        conv_kernel,
        in_specs=[whole] * 6,
        out_specs=[whole] * 3,
        out_shape=[jax.ShapeDtypeStruct(chunks.shape, jnp.bfloat16), plane, plane],
        scratch_shapes=[
            pltpu.VMEM((size, 2 * TILE), jnp.bfloat16),
            pltpu.VMEM((size, 4 * TILE), jnp.float8_e4m3fn),
            pltpu.VMEM((count * 4, TILE), jnp.float32),
            pltpu.VMEM(tiles, jnp.bfloat16),
            pltpu.VMEM(tiles, jnp.float8_e4m3fn),
            pltpu.VMEM(tiles, jnp.float8_e4m3fn),
            pltpu.VMEM((size, 2 * TILE), jnp.float32),
            pltpu.VMEM((ROWS, TILE), jnp.float32),
            pltpu.VMEM((count, TILE), jnp.float32),
            pltpu.VMEM((count + 8, TILE), jnp.float32),
            pltpu.VMEM((count, TILE), jnp.float32),
            pltpu.VMEM((count, TILE), jnp.float32),
            pltpu.VMEM((count, TILE), jnp.float32),
        ],
        compiler_params=pltpu.CompilerParams(vmem_limit_bytes=24 * MIB),
        name="conv",
    )(chunks, *streams, weight, skip)


def back_kernel(in_ref, query_ref, base_ref, out_ref, plain, starts):
    lane = lax.broadcasted_iota(jnp.int32, (ROWS, TILE), 1)
    row = lax.broadcasted_iota(jnp.int32, (ROWS, TILE), 0)
    step = pl.program_id(0)
    for filt in range(FILT):
        src = step * FILT + filt
        tail = in_ref[src, pl.ds(64, 8), :].astype(jnp.float32)
        scale = jnp.sum(jnp.where(lane == row, tail[0:1, :], 0.0), axis=1, keepdims=True)
        zero = jnp.sum(jnp.where(lane == row, tail[1:2, :], 0.0), axis=1, keepdims=True)
        one = jnp.sum(jnp.where(lane == row + ROWS, tail[1:2, :], 0.0), axis=1, keepdims=True)
        starts[pl.ds(filt, ROWS, stride=FILT), :] = jnp.where(lane == 0, zero, one)
        for block in range(4):
            part = in_ref[src, pl.ds(block * ROWS, ROWS), :].astype(jnp.float32)
            plain[block, pl.ds(filt, ROWS, stride=FILT), :] = decode(part, scale)
    rows = pl.ds(pl.multiple_of(step * TILE, TILE), TILE)
    long = jnp.concatenate([plain[block] for block in range(4)], axis=1)
    mixed = query_ref[rows, :] * long + base_ref[rows, :]
    head = lax.broadcasted_iota(jnp.int32, (TILE, TILE), 1)
    out_ref[:, :TILE] = jnp.where(head < 2, starts[...], mixed[:, :TILE]).astype(jnp.bfloat16)
    out_ref[:, TILE:] = mixed[:, TILE:].astype(jnp.bfloat16)


WHOLE = pl.BlockSpec(memory_space=pltpu.VMEM)


def whole_call(kernel, name, outs, *operands):
    return pl.pallas_call(
        kernel,
        in_specs=[WHOLE] * len(operands),
        out_specs=[WHOLE] * len(outs),
        out_shape=[jax.ShapeDtypeStruct(shape, dtype) for shape, dtype in outs],
        compiler_params=pltpu.CompilerParams(vmem_limit_bytes=16 * MIB),
        name=name,
    )(*operands)


def back(chunks, query_short, base):
    rows, length = base.shape
    return pl.pallas_call(
        back_kernel,
        grid=(rows // TILE,),
        in_specs=[WHOLE] * 3,
        out_specs=pl.BlockSpec((TILE, length), lambda n: (n, 0)),
        out_shape=jax.ShapeDtypeStruct((rows, length), jnp.bfloat16),
        scratch_shapes=[
            pltpu.VMEM((4, TILE, TILE), jnp.float32),
            pltpu.VMEM((TILE, TILE), jnp.float32),
        ],
        compiler_params=pltpu.CompilerParams(vmem_limit_bytes=16 * MIB),
        name="back",
    )(chunks, query_short, base)


def local(query_proj, key_proj, value_proj, short_weight, skip_bias, filter_taps):
    count = lax.axis_size("context")
    rows, length = query_proj.shape
    taps = jnp.broadcast_to(filter_taps[:, None, :], (FILT, 1, length))
    taps = lax.all_to_all(taps, "tensor", 0, 0, tiled=True)
    weight = short_weight.reshape(9, rows)
    skip = skip_bias[None, :]
    outs = [
        ((4, rows, TILE), jnp.float32),
        ((count, TILE), jnp.float32),
        ((2, count, TILE), jnp.float32),
    ]
    streams = (key_proj, value_proj, query_proj)
    coded, scales, ends = whole_call(front_kernel, "front", outs, *streams, weight)
    outs = [((count, CHUNK, TILE), jnp.bfloat16)]
    (chunks,) = whole_call(deal_kernel, "deal", outs, coded, scales, ends, taps)
    chunks = lax.all_to_all(chunks, "context", 0, 0, tiled=True)
    streams = (query_proj, key_proj, value_proj)
    chunks, query_short, base = conv(chunks, streams, weight, skip)
    chunks = lax.all_to_all(chunks, "context", 0, 0, tiled=True)
    return back(chunks, query_short, base)


def solution(mesh):
    in_specs = (
        P("tensor", "context"),
        P("tensor", "context"),
        P("tensor", "context"),
        P(None, None, "tensor"),
        P("tensor"),
        P("tensor", "context"),
    )
    out_specs = P("tensor", "context")
    return jax.shard_map(local, mesh=mesh, in_specs=in_specs, out_specs=out_specs, check_vma=False)
```

time: 82.9 us -> 80.1 us (0.966)
  local copies, waits for them, and re-layouts: 1.29 us -> 4.46 us
  starting transfers between devices: 8.31 us -> 5.43 us
  Pallas kernels: 19 us -> 16.8 us
    ppermute x1 -> x0, starting transfers between devices: 3.4 us -> none  [local(): rim = lax.ppermute(rim, 'context', [(n, n + 1) for n in range(count - 1)])]
    unnamed x12 -> x16, local copies, waits for them, and re-layouts: 0.66 us -> 3.15 us
    pallas_call x2 -> x1, Pallas kernels: 14 us -> 11.9 us  [conv(): pl.pallas_call(conv_kernel, in_specs=[whole] * 6, out_specs=[whole] * 3,...]
  transfers between devices with their start and end apart: 2 -> 1, of which waited for: 1 -> 0; matrix products, arithmetic and copies ran while one was open for 1% -> 0% of each run, Pallas kernels for 3% -> 3%
where the time goes in v3:
time: 80.1 us; the launch traced here: 79.7 us
  blocking collectives  52.9 us (66%)
  Pallas kernels  16.8 us (21%)
  starting transfers between devices  5.43 us (7%)
  local copies, waits for them, and re-layouts  4.46 us (6%)
    all_to_all x2, blocking collectives, local(): chunks = lax.all_to_all(chunks, 'context', 0, 0, tiled=True)  52.9 us
    pallas_call x1, Pallas kernels, conv(): pl.pallas_call(conv_kernel, in_specs=[whole] * 6, out_specs=[whole] * 3,...  11.9 us
    all_to_all x1, starting transfers between devices, local(): taps = lax.all_to_all(taps, 'tensor', 0, 0, tiled=True)  5.43 us
    unnamed x16, local copies, waits for them, and re-layouts  3.15 us
    pallas_call x2, Pallas kernels, whole_call(): pl.pallas_call(kernel, in_specs=[WHOLE] * len(operands), out_specs=[WHOLE...  2.87 us
    pallas_call x1, Pallas kernels, back(): pl.pallas_call(back_kernel, grid=(rows // TILE,), in_specs=[WHOLE] * 3, o...  2.03 us
  transfers between devices with their start and end apart: 1, of which 0 were waited for; matrix products, arithmetic and copies ran while one was open for 0% of the time, Pallas kernels for 3%

profile of v3, /device:TPU:8, one launch (start us, length us, event | category | flops | bytes accessed | tf_op | source)
XLA Modules:
  0.0 79.7 jit_solution(13430640995014476230)
XLA Ops:
  0.0 0.0 copy-start.7
  0.0 1.3 %broadcast_in_dim.12 = f32[8,1,512]{2,1,0:T(1,128)} broadcast(f32[512]{0:T(512)} %bitcast.3), dimensions={2} | broadcast | bytes 18432 | tf_op jit(solution)/shard_map/broadcast_in_dim | solution.py:442
  1.3 5.4 %all-to-all-start = ((f32[8,1,512]{2,1,0:T(1,128)}), f32[8,1,512]{2,1,0:T(1,128)S(1)}, u32[]{:S(2)}, u32[]{:S(2)}) async-start(f32[8,1,512]{2,1,0:T(1,128)} %broadcast_in_dim.12), calls=%async_computation | async-start | bytes 32768 | tf_op jit(solution)/shard_map/all_to_all | solution.py:443
  6.7 0.0 copy-done.7
  6.8 0.0 copy-start
  6.8 1.0 %copy-done = bf16[512,512]{1,0:T(8,128)(2,1)S(1)} copy-done((bf16[512,512]{1,0:T(8,128)(2,1)S(1)}, bf16[512,512]{1,0:T(8,128)(2,1)}, u32[]{:S(2)}) %copy-start) | copy-done | bytes 524312
  7.8 0.0 copy-start.2
  7.8 1.0 %copy-done.2 = bf16[512,512]{1,0:T(8,128)(2,1)S(1)} copy-done((bf16[512,512]{1,0:T(8,128)(2,1)S(1)}, bf16[512,512]{1,0:T(8,128)(2,1)}, u32[]{:S(2)}) %copy-start.2) | copy-done | bytes 524312
  8.8 0.0 copy-start.4
  8.8 1.0 %copy-done.4 = bf16[512,512]{1,0:T(8,128)(2,1)S(1)} copy-done((bf16[512,512]{1,0:T(8,128)(2,1)S(1)}, bf16[512,512]{1,0:T(8,128)(2,1)}, u32[]{:S(2)}) %copy-start.4) | copy-done | bytes 524312
  9.9 2.2 %front.1 = (f32[4,512,128]{2,1,0:T(8,128)S(1)}, f32[32,128]{1,0:T(8,128)S(1)}, f32[2,32,128]{2,1,0:T(8,128)S(1)}) custom-call(bf16[512,512]{1,0:T(8,128)(2,1)S(1)} %copy-done, bf16[512,512]{1,0:T(8,128)(2,1)S(1)} %copy-done.2, bf16[512,512]{1,0:T(8,128)(2,1)S(1)} %copy-done.4, f32[9,512]{1,0:T(8,128)S(1)} %reshape.6.weight_ref), custom_call_target="tpu_custom_call" | custom-call | tf_op jit(solution)/shard_map/front/pallas_call | solution.py:412
  12.1 0.0 all-to-all-done.taps_ref
  12.1 0.0 copy-start.5
  12.1 0.7 deal.1
  12.8 0.0 copy-start.1
  12.8 0.0 copy-start.3
  12.8 0.0 copy-start.6
  12.8 30.1 %all_to_all.15.in_ref = bf16[32,72,128]{2,1,0:T(8,128)(2,1)S(1)} all-to-all(bf16[32,72,128]{2,1,0:T(8,128)(2,1)S(1)} %deal.1), channel_id=1, replica_groups=mesh['context'=32,'tensor'=8] {'context'}, dimensions={0} | all-to-all | bytes 1179648 | tf_op jit(solution)/shard_map/all_to_all | solution.py:455
  42.9 0.0 copy-done.5
  42.9 0.0 copy-done.1
  42.9 0.0 copy-done.3
  42.9 0.0 copy-done.6
  42.9 11.9 %conv.1 = (bf16[32,72,128]{2,1,0:T(8,128)(2,1)S(1)}, f32[512,512]{1,0:T(8,128)S(1)}, f32[512,512]{1,0:T(8,128)S(1)}) custom-call(bf16[32,72,128]{2,1,0:T(8,128)(2,1)S(1)} %all_to_all.15.in_ref, bf16[512,512]{1,0:T(8,128)(2,1)S(1)} %copy-done.5, bf16[512,512]{1,0:T(8,128)(2,1)S(1)} %copy-done.1, bf16[512,512]{1,0:T(8,128)(2,1)S(1)} %copy-done.3, ...), custom_call_target="tpu_custom_call" | custom-call | tf_op jit(solution)/shard_map/conv/pallas_call | solution.py:361
  54.8 22.8 %all_to_all.16.in_ref = bf16[32,72,128]{2,1,0:T(8,128)(2,1)S(1)} all-to-all(bf16[32,72,128]{2,1,0:T(8,128)(2,1)S(1)} %get-tuple-element.14), channel_id=1, replica_groups=mesh['context'=32,'tensor'=8] {'context'}, dimensions={0} | all-to-all | bytes 1179648 | tf_op jit(solution)/shard_map/all_to_all | solution.py:458
  77.6 2.0 %back.1 = bf16[512,512]{1,0:T(8,128)(2,1)} custom-call(bf16[32,72,128]{2,1,0:T(8,128)(2,1)S(1)} %all_to_all.16.in_ref, f32[512,512]{1,0:T(8,128)S(1)} %get-tuple-element.15.query_ref, f32[512,512]{1,0:T(8,128)S(1)} %get-tuple-element.16.base_ref), custom_call_target="tpu_custom_call" | custom-call | tf_op jit(solution)/shard_map/back/pallas_call | solution.py:424
  (1 shorter events, 0.0 us)
Async XLA Ops:
  0.0 6.7 %copy-start.7 = (f32[3,3,512]{2,1,0:T(4,128)S(1)}, f32[3,3,512]{2,1,0:T(4,128)}, u32[]{:S(2)}) copy-start(f32[3,3,512]{2,1,0:T(4,128)} %param.9) | copy-start | bytes 55300
  1.3 10.8 %all-to-all-start = ((f32[8,1,512]{2,1,0:T(1,128)}), f32[8,1,512]{2,1,0:T(1,128)S(1)}, u32[]{:S(2)}, u32[]{:S(2)}) async-start(f32[8,1,512]{2,1,0:T(1,128)} %broadcast_in_dim.12), calls=%async_computation | async-start | bytes 32768 | tf_op jit(solution)/shard_map/all_to_all | solution.py:443
  6.8 1.0 %copy-start = (bf16[512,512]{1,0:T(8,128)(2,1)S(1)}, bf16[512,512]{1,0:T(8,128)(2,1)}, u32[]{:S(2)}) copy-start(bf16[512,512]{1,0:T(8,128)(2,1)} %key_ref.3) | copy-start | bytes 1572868
  7.8 1.0 %copy-start.2 = (bf16[512,512]{1,0:T(8,128)(2,1)S(1)}, bf16[512,512]{1,0:T(8,128)(2,1)}, u32[]{:S(2)}) copy-start(bf16[512,512]{1,0:T(8,128)(2,1)} %value_ref.3) | copy-start | bytes 1572868
  8.8 1.0 %copy-start.4 = (bf16[512,512]{1,0:T(8,128)(2,1)S(1)}, bf16[512,512]{1,0:T(8,128)(2,1)}, u32[]{:S(2)}) copy-start(bf16[512,512]{1,0:T(8,128)(2,1)} %query_ref.3) | copy-start | bytes 1572868
  12.1 30.8 %copy-start.5 = (bf16[512,512]{1,0:T(8,128)(2,1)S(1)}, bf16[512,512]{1,0:T(8,128)(2,1)}, u32[]{:S(2)}) copy-start(bf16[512,512]{1,0:T(8,128)(2,1)} %query_ref.3) | copy-start | bytes 1572868
  12.8 30.1 %copy-start.1 = (bf16[512,512]{1,0:T(8,128)(2,1)S(1)}, bf16[512,512]{1,0:T(8,128)(2,1)}, u32[]{:S(2)}) copy-start(bf16[512,512]{1,0:T(8,128)(2,1)} %key_ref.3) | copy-start | bytes 1572868
  12.8 30.1 %copy-start.3 = (bf16[512,512]{1,0:T(8,128)(2,1)S(1)}, bf16[512,512]{1,0:T(8,128)(2,1)}, u32[]{:S(2)}) copy-start(bf16[512,512]{1,0:T(8,128)(2,1)} %value_ref.3) | copy-start | bytes 1572868
  12.8 30.1 %copy-start.6 = (f32[512]{0:T(512)S(1)}, f32[512]{0:T(512)}, u32[]{:S(2)}) copy-start(f32[512]{0:T(512)} %param.10) | copy-start | bytes 6148

commit v4 on v3

--- a/solution.py
+++ b/solution.py
@@ -139,10 +139,10 @@
 
 
 FINE = 512.0
-GATE_FROM = 2
-GATE_STEP = 2
-EARLY = 12
-PER_STEP = 3
+GATE_FROM = 0
+GATE_STEP = 1
+EARLY = 4
+PER_STEP = 8
 
 
 def unit_of(peak):
@@ -383,26 +383,35 @@
     )(chunks, *streams, weight, skip)
 
 
-def back_kernel(in_ref, query_ref, base_ref, out_ref, plain, starts):
+def back_kernel(in_ref, query_ref, base_ref, out_hbm, plain, starts, done, sent):
     lane = lax.broadcasted_iota(jnp.int32, (ROWS, TILE), 1)
     row = lax.broadcasted_iota(jnp.int32, (ROWS, TILE), 0)
-    step = pl.program_id(0)
-    for filt in range(FILT):
-        src = step * FILT + filt
-        tail = in_ref[src, pl.ds(64, 8), :].astype(jnp.float32)
-        scale = jnp.sum(jnp.where(lane == row, tail[0:1, :], 0.0), axis=1, keepdims=True)
-        zero = jnp.sum(jnp.where(lane == row, tail[1:2, :], 0.0), axis=1, keepdims=True)
-        one = jnp.sum(jnp.where(lane == row + ROWS, tail[1:2, :], 0.0), axis=1, keepdims=True)
-        starts[pl.ds(filt, ROWS, stride=FILT), :] = jnp.where(lane == 0, zero, one)
-        for block in range(4):
-            part = in_ref[src, pl.ds(block * ROWS, ROWS), :].astype(jnp.float32)
-            plain[block, pl.ds(filt, ROWS, stride=FILT), :] = decode(part, scale)
-    rows = pl.ds(pl.multiple_of(step * TILE, TILE), TILE)
-    long = jnp.concatenate([plain[block] for block in range(4)], axis=1)
-    mixed = query_ref[rows, :] * long + base_ref[rows, :]
     head = lax.broadcasted_iota(jnp.int32, (TILE, TILE), 1)
-    out_ref[:, :TILE] = jnp.where(head < 2, starts[...], mixed[:, :TILE]).astype(jnp.bfloat16)
-    out_ref[:, TILE:] = mixed[:, TILE:].astype(jnp.bfloat16)
+    copies = []
+    for step in range(done.shape[0] // TILE):
+        for filt in range(FILT):
+            src = step * FILT + filt
+            tail = in_ref[src, pl.ds(64, 8), :].astype(jnp.float32)
+            scale = jnp.sum(jnp.where(lane == row, tail[0:1, :], 0.0), axis=1, keepdims=True)
+            zero = jnp.sum(jnp.where(lane == row, tail[1:2, :], 0.0), axis=1, keepdims=True)
+            one = jnp.where(lane == row + ROWS, tail[1:2, :], 0.0)
+            one = jnp.sum(one, axis=1, keepdims=True)
+            starts[step, pl.ds(filt, ROWS, stride=FILT), :] = jnp.where(lane == 0, zero, one)
+            for block in range(4):
+                part = in_ref[src, pl.ds(block * ROWS, ROWS), :].astype(jnp.float32)
+                plain[step, block, pl.ds(filt, ROWS, stride=FILT), :] = decode(part, scale)
+        rows = pl.ds(step * TILE, TILE)
+        for block in range(4):
+            cols = pl.ds(block * TILE, TILE)
+            mixed = query_ref[rows, cols] * plain[step, block] + base_ref[rows, cols]
+            if block == 0:
+                mixed = jnp.where(head < 2, starts[step], mixed)
+            done[rows, cols] = mixed.astype(jnp.bfloat16)
+        copy = pltpu.make_async_copy(done.at[rows, :], out_hbm.at[rows, :], sent.at[step])
+        copy.start()
+        copies.append(copy)
+    for copy in copies:
+        copy.wait()
 
 
 WHOLE = pl.BlockSpec(memory_space=pltpu.VMEM)
@@ -421,15 +430,17 @@
 
 def back(chunks, query_short, base):
     rows, length = base.shape
+    steps = rows // TILE
     return pl.pallas_call(
         back_kernel,
-        grid=(rows // TILE,),
         in_specs=[WHOLE] * 3,
-        out_specs=pl.BlockSpec((TILE, length), lambda n: (n, 0)),
+        out_specs=pl.BlockSpec(memory_space=pl.ANY),
         out_shape=jax.ShapeDtypeStruct((rows, length), jnp.bfloat16),
         scratch_shapes=[
-            pltpu.VMEM((4, TILE, TILE), jnp.float32),
-            pltpu.VMEM((TILE, TILE), jnp.float32),
+            pltpu.VMEM((steps, 4, TILE, TILE), jnp.float32),
+            pltpu.VMEM((steps, TILE, TILE), jnp.float32),
+            pltpu.VMEM((rows, length), jnp.bfloat16),
+            pltpu.SemaphoreType.DMA((steps,)),
         ],
         compiler_params=pltpu.CompilerParams(vmem_limit_bytes=16 * MIB),
         name="back",

time: 80.1 us -> 79.5 us (level)
  no operation moved by 1% of the time
where the time goes in v4:
time: 79.5 us; the launch traced here: 79.1 us
  blocking collectives  52.9 us (67%)
  Pallas kernels  16 us (20%)
  starting transfers between devices  5.43 us (7%)
  local copies, waits for them, and re-layouts  4.46 us (6%)
    all_to_all x2, blocking collectives, local(): chunks = lax.all_to_all(chunks, 'context', 0, 0, tiled=True)  52.9 us
    pallas_call x1, Pallas kernels, conv(): pl.pallas_call(conv_kernel, in_specs=[whole] * 6, out_specs=[whole] * 3,...  11.7 us
    all_to_all x1, starting transfers between devices, local(): taps = lax.all_to_all(taps, 'tensor', 0, 0, tiled=True)  5.43 us
    unnamed x16, local copies, waits for them, and re-layouts  3.15 us
    pallas_call x2, Pallas kernels, whole_call(): pl.pallas_call(kernel, in_specs=[WHOLE] * len(operands), out_specs=[WHOLE...  2.87 us
  transfers between devices with their start and end apart: 1, of which 0 were waited for; matrix products, arithmetic and copies ran while one was open for 0% of the time, Pallas kernels for 3%

profile of v4, /device:TPU:8, one launch (start us, length us, event | category | flops | bytes accessed | tf_op | source)
XLA Modules:
  0.0 79.1 jit_solution(2424935848661469154)
XLA Ops:
  0.0 0.0 copy-start.7
  0.0 1.3 %broadcast_in_dim.12 = f32[8,1,512]{2,1,0:T(1,128)} broadcast(f32[512]{0:T(512)} %bitcast.3), dimensions={2} | broadcast | bytes 18432 | tf_op jit(solution)/shard_map/broadcast_in_dim | solution.py:453
  1.3 5.4 %all-to-all-start = ((f32[8,1,512]{2,1,0:T(1,128)}), f32[8,1,512]{2,1,0:T(1,128)S(1)}, u32[]{:S(2)}, u32[]{:S(2)}) async-start(f32[8,1,512]{2,1,0:T(1,128)} %broadcast_in_dim.12), calls=%async_computation | async-start | bytes 32768 | tf_op jit(solution)/shard_map/all_to_all | solution.py:454
  6.7 0.0 copy-done.7
  6.8 0.0 copy-start
  6.8 1.0 %copy-done = bf16[512,512]{1,0:T(8,128)(2,1)S(1)} copy-done((bf16[512,512]{1,0:T(8,128)(2,1)S(1)}, bf16[512,512]{1,0:T(8,128)(2,1)}, u32[]{:S(2)}) %copy-start) | copy-done | bytes 524312
  7.8 0.0 copy-start.2
  7.8 1.0 %copy-done.2 = bf16[512,512]{1,0:T(8,128)(2,1)S(1)} copy-done((bf16[512,512]{1,0:T(8,128)(2,1)S(1)}, bf16[512,512]{1,0:T(8,128)(2,1)}, u32[]{:S(2)}) %copy-start.2) | copy-done | bytes 524312
  8.8 0.0 copy-start.4
  8.8 1.0 %copy-done.4 = bf16[512,512]{1,0:T(8,128)(2,1)S(1)} copy-done((bf16[512,512]{1,0:T(8,128)(2,1)S(1)}, bf16[512,512]{1,0:T(8,128)(2,1)}, u32[]{:S(2)}) %copy-start.4) | copy-done | bytes 524312
  9.9 2.2 %front.1 = (f32[4,512,128]{2,1,0:T(8,128)S(1)}, f32[32,128]{1,0:T(8,128)S(1)}, f32[2,32,128]{2,1,0:T(8,128)S(1)}) custom-call(bf16[512,512]{1,0:T(8,128)(2,1)S(1)} %copy-done, bf16[512,512]{1,0:T(8,128)(2,1)S(1)} %copy-done.2, bf16[512,512]{1,0:T(8,128)(2,1)S(1)} %copy-done.4, f32[9,512]{1,0:T(8,128)S(1)} %reshape.6.weight_ref), custom_call_target="tpu_custom_call" | custom-call | tf_op jit(solution)/shard_map/front/pallas_call | solution.py:421
  12.1 0.0 all-to-all-done.taps_ref
  12.1 0.0 copy-start.5
  12.1 0.7 deal.1
  12.8 0.0 copy-start.1
  12.8 0.0 copy-start.3
  12.8 0.0 copy-start.6
  12.8 30.1 %all_to_all.15.in_ref = bf16[32,72,128]{2,1,0:T(8,128)(2,1)S(1)} all-to-all(bf16[32,72,128]{2,1,0:T(8,128)(2,1)S(1)} %deal.1), channel_id=1, replica_groups=mesh['context'=32,'tensor'=8] {'context'}, dimensions={0} | all-to-all | bytes 1179648 | tf_op jit(solution)/shard_map/all_to_all | solution.py:466
  42.9 0.0 copy-done.5
  42.9 0.0 copy-done.1
  42.9 0.0 copy-done.3
  42.9 0.0 copy-done.6
  42.9 11.7 %conv.1 = (bf16[32,72,128]{2,1,0:T(8,128)(2,1)S(1)}, f32[512,512]{1,0:T(8,128)S(1)}, f32[512,512]{1,0:T(8,128)S(1)}) custom-call(bf16[32,72,128]{2,1,0:T(8,128)(2,1)S(1)} %all_to_all.15.in_ref, bf16[512,512]{1,0:T(8,128)(2,1)S(1)} %copy-done.5, bf16[512,512]{1,0:T(8,128)(2,1)S(1)} %copy-done.1, bf16[512,512]{1,0:T(8,128)(2,1)S(1)} %copy-done.3, ...), custom_call_target="tpu_custom_call" | custom-call | tf_op jit(solution)/shard_map/conv/pallas_call | solution.py:361
  54.6 22.8 %all_to_all.16.in_ref = bf16[32,72,128]{2,1,0:T(8,128)(2,1)S(1)} all-to-all(bf16[32,72,128]{2,1,0:T(8,128)(2,1)S(1)} %get-tuple-element.14), channel_id=1, replica_groups=mesh['context'=32,'tensor'=8] {'context'}, dimensions={0} | all-to-all | bytes 1179648 | tf_op jit(solution)/shard_map/all_to_all | solution.py:469
  77.4 1.5 %back.1 = bf16[512,512]{1,0:T(8,128)(2,1)} custom-call(bf16[32,72,128]{2,1,0:T(8,128)(2,1)S(1)} %all_to_all.16.in_ref, f32[512,512]{1,0:T(8,128)S(1)} %get-tuple-element.15.query_ref, f32[512,512]{1,0:T(8,128)S(1)} %get-tuple-element.16.base_ref), custom_call_target="tpu_custom_call" | custom-call | tf_op jit(solution)/shard_map/back/pallas_call | solution.py:434
  (1 shorter events, 0.0 us)
Async XLA Ops:
  0.0 6.7 %copy-start.7 = (f32[3,3,512]{2,1,0:T(4,128)S(1)}, f32[3,3,512]{2,1,0:T(4,128)}, u32[]{:S(2)}) copy-start(f32[3,3,512]{2,1,0:T(4,128)} %param.9) | copy-start | bytes 55300
  1.3 10.8 %all-to-all-start = ((f32[8,1,512]{2,1,0:T(1,128)}), f32[8,1,512]{2,1,0:T(1,128)S(1)}, u32[]{:S(2)}, u32[]{:S(2)}) async-start(f32[8,1,512]{2,1,0:T(1,128)} %broadcast_in_dim.12), calls=%async_computation | async-start | bytes 32768 | tf_op jit(solution)/shard_map/all_to_all | solution.py:454
  6.8 1.0 %copy-start = (bf16[512,512]{1,0:T(8,128)(2,1)S(1)}, bf16[512,512]{1,0:T(8,128)(2,1)}, u32[]{:S(2)}) copy-start(bf16[512,512]{1,0:T(8,128)(2,1)} %key_ref.3) | copy-start | bytes 1572868
  7.8 1.0 %copy-start.2 = (bf16[512,512]{1,0:T(8,128)(2,1)S(1)}, bf16[512,512]{1,0:T(8,128)(2,1)}, u32[]{:S(2)}) copy-start(bf16[512,512]{1,0:T(8,128)(2,1)} %value_ref.3) | copy-start | bytes 1572868
  8.8 1.0 %copy-start.4 = (bf16[512,512]{1,0:T(8,128)(2,1)S(1)}, bf16[512,512]{1,0:T(8,128)(2,1)}, u32[]{:S(2)}) copy-start(bf16[512,512]{1,0:T(8,128)(2,1)} %query_ref.3) | copy-start | bytes 1572868
  12.1 30.8 %copy-start.5 = (bf16[512,512]{1,0:T(8,128)(2,1)S(1)}, bf16[512,512]{1,0:T(8,128)(2,1)}, u32[]{:S(2)}) copy-start(bf16[512,512]{1,0:T(8,128)(2,1)} %query_ref.3) | copy-start | bytes 1572868
  12.8 30.1 %copy-start.1 = (bf16[512,512]{1,0:T(8,128)(2,1)S(1)}, bf16[512,512]{1,0:T(8,128)(2,1)}, u32[]{:S(2)}) copy-start(bf16[512,512]{1,0:T(8,128)(2,1)} %key_ref.3) | copy-start | bytes 1572868
  12.8 30.1 %copy-start.3 = (bf16[512,512]{1,0:T(8,128)(2,1)S(1)}, bf16[512,512]{1,0:T(8,128)(2,1)}, u32[]{:S(2)}) copy-start(bf16[512,512]{1,0:T(8,128)(2,1)} %value_ref.3) | copy-start | bytes 1572868
  12.8 30.1 %copy-start.6 = (f32[512]{0:T(512)S(1)}, f32[512]{0:T(512)}, u32[]{:S(2)}) copy-start(f32[512]{0:T(512)} %param.10) | copy-start | bytes 6148

commit v5 on v4

--- a/solution.py
+++ b/solution.py
@@ -66,13 +66,13 @@
     return key_short * value_short
 
 
-def ends_of(refs, start):
+def ends_of(refs, start, base):
     shape = (TILE, TILE)
     lane = lax.broadcasted_iota(jnp.int32, shape, 1)
     place = lax.broadcasted_iota(jnp.int32, shape, 0)
     total = None
     for index, ref in enumerate(refs):
-        pick = (lane // 32 == index) & (place == start % TILE + lane % 32 // 16)
+        pick = (lane // 32 == base + index) & (place == start % TILE + lane % 32 // 16)
         part = jnp.dot(
             ref[:, start // TILE * TILE : start // TILE * TILE + TILE],
             pick.astype(jnp.bfloat16),
@@ -82,19 +82,24 @@
     return total
 
 
-def front_kernel(key_ref, value_ref, query_ref, weight_ref, coded_ref, scale_ref, ends_ref):
-    length = key_ref.shape[1]
-    refs = (key_ref, value_ref, query_ref)
+def ends_rows(both, step):
     group = lax.broadcasted_iota(jnp.int32, (TILE, TILE), 0) // FILT
     own = lax.broadcasted_iota(jnp.int32, (TILE, TILE), 1) % ROWS == group
+    rows = slice(step * TILE, (step + 1) * TILE)
+    spread = [jnp.where(own, part[rows, :], 0.0) for part in both]
+    return [part.reshape(ROWS, FILT, TILE).sum(axis=0) for part in spread]
+
+
+def front_kernel(key_ref, value_ref, weight_ref, coded_ref, scale_ref, ends_ref):
+    length = key_ref.shape[1]
+    refs = (key_ref, value_ref)
     lane = lax.broadcasted_iota(jnp.int32, (TILE, length), 1)
-    both = [ends_of(refs, 0), ends_of(refs, length - 2)]
+    both = [ends_of(refs, start, 0) for start in (0, length - 2)]
     for step in range(key_ref.shape[0] // TILE):
         rows = slice(step * TILE, (step + 1) * TILE)
         dests = slice(step * FILT, (step + 1) * FILT)
-        for which in range(2):
-            spread = jnp.where(own, both[which][rows, :], 0.0)
-            ends_ref[which, dests, :] = spread.reshape(ROWS, FILT, TILE).sum(axis=0)
+        for which, part in enumerate(ends_rows(both, step)):
+            ends_ref[which, dests, :] = part
         side = side_columns([weight_ref[:, rows]])
         product = jnp.where(lane < 2, 0.0, product_of(key_ref, value_ref, side, rows))
         scale = scale_of(jnp.max(jnp.abs(product), axis=1, keepdims=True))
@@ -104,7 +109,8 @@
         scale_ref[dests, :] = to_lanes(scale)
 
 
-def deal_kernel(coded_ref, scale_ref, ends_ref, taps_ref, out_ref):
+def deal_kernel(coded_ref, scale_ref, ends_ref, query_ref, taps_ref, out_ref):
+    both = [ends_of((query_ref,), start, 2) for start in (0, query_ref.shape[1] - 2)]
     row = lax.broadcasted_iota(jnp.int32, (8, TILE), 0)
     tails = []
     for filt in range(FILT):
@@ -118,13 +124,17 @@
         tails.append(tail)
     for dest in range(out_ref.shape[0]):
         step, filt = dest // FILT, dest % FILT
+        if filt == 0:
+            late = ends_rows(both, step)
         for block in range(4):
             rows = pl.ds(step * TILE + filt, ROWS, stride=FILT)
             part = coded_ref[block, rows, :]
             out_ref[dest, block * ROWS : (block + 1) * ROWS, :] = part.astype(jnp.bfloat16)
         tail = jnp.where(row == 4, scale_ref[dest : dest + 1, :], tails[filt])
-        tail = jnp.where(row == 6, ends_ref[0, dest : dest + 1, :], tail)
-        tail = jnp.where(row == 7, ends_ref[1, dest : dest + 1, :], tail)
+        ends = ends_ref[0, dest : dest + 1, :] + late[0][filt : filt + 1, :]
+        tail = jnp.where(row == 6, ends, tail)
+        ends = ends_ref[1, dest : dest + 1, :] + late[1][filt : filt + 1, :]
+        tail = jnp.where(row == 7, ends, tail)
         out_ref[dest, 64:72, :] = tail.astype(jnp.bfloat16)
 
 
@@ -459,10 +469,10 @@
         ((count, TILE), jnp.float32),
         ((2, count, TILE), jnp.float32),
     ]
-    streams = (key_proj, value_proj, query_proj)
+    streams = (key_proj, value_proj)
     coded, scales, ends = whole_call(front_kernel, "front", outs, *streams, weight)
     outs = [((count, CHUNK, TILE), jnp.bfloat16)]
-    (chunks,) = whole_call(deal_kernel, "deal", outs, coded, scales, ends, taps)
+    (chunks,) = whole_call(deal_kernel, "deal", outs, coded, scales, ends, query_proj, taps)
     chunks = lax.all_to_all(chunks, "context", 0, 0, tiled=True)
     streams = (query_proj, key_proj, value_proj)
     chunks, query_short, base = conv(chunks, streams, weight, skip)

time: 79.5 us -> 78.3 us (0.985)
  local copies, waits for them, and re-layouts: 4.46 us -> 3.42 us
    unnamed x16 -> x14, local copies, waits for them, and re-layouts: 3.15 us -> 2.1 us
where the time goes in v5:
time: 78.3 us; the launch traced here: 78 us
  blocking collectives  52.9 us (68%)
  Pallas kernels  16 us (20%)
  starting transfers between devices  5.43 us (7%)
  local copies, waits for them, and re-layouts  3.42 us (4%)
    all_to_all x2, blocking collectives, local(): chunks = lax.all_to_all(chunks, 'context', 0, 0, tiled=True)  52.9 us
    pallas_call x1, Pallas kernels, conv(): pl.pallas_call(conv_kernel, in_specs=[whole] * 6, out_specs=[whole] * 3,...  11.7 us
    all_to_all x1, starting transfers between devices, local(): taps = lax.all_to_all(taps, 'tensor', 0, 0, tiled=True)  5.43 us
    pallas_call x2, Pallas kernels, whole_call(): pl.pallas_call(kernel, in_specs=[WHOLE] * len(operands), out_specs=[WHOLE...  2.83 us
    unnamed x14, local copies, waits for them, and re-layouts  2.1 us
  transfers between devices with their start and end apart: 1, of which 0 were waited for; matrix products, arithmetic and copies ran while one was open for 0% of the time, Pallas kernels for 3%

profile of v5, /device:TPU:8, one launch (start us, length us, event | category | flops | bytes accessed | tf_op | source)
XLA Modules:
  0.0 78.0 jit_solution(5386982161468908295)
XLA Ops:
  0.0 0.0 copy-start.6
  0.0 1.3 %broadcast_in_dim.12 = f32[8,1,512]{2,1,0:T(1,128)} broadcast(f32[512]{0:T(512)} %bitcast.3), dimensions={2} | broadcast | bytes 18432 | tf_op jit(solution)/shard_map/broadcast_in_dim | solution.py:463
  1.3 5.4 %all-to-all-start = ((f32[8,1,512]{2,1,0:T(1,128)}), f32[8,1,512]{2,1,0:T(1,128)S(1)}, u32[]{:S(2)}, u32[]{:S(2)}) async-start(f32[8,1,512]{2,1,0:T(1,128)} %broadcast_in_dim.12), calls=%async_computation | async-start | bytes 32768 | tf_op jit(solution)/shard_map/all_to_all | solution.py:464
  6.7 0.0 copy-done.6
  6.8 0.0 copy-start.1
  6.8 1.0 %copy-done.1 = bf16[512,512]{1,0:T(8,128)(2,1)S(1)} copy-done((bf16[512,512]{1,0:T(8,128)(2,1)S(1)}, bf16[512,512]{1,0:T(8,128)(2,1)}, u32[]{:S(2)}) %copy-start.1) | copy-done | bytes 524312
  7.8 0.0 copy-start.3
  7.8 1.0 %copy-done.3 = bf16[512,512]{1,0:T(8,128)(2,1)S(1)} copy-done((bf16[512,512]{1,0:T(8,128)(2,1)S(1)}, bf16[512,512]{1,0:T(8,128)(2,1)}, u32[]{:S(2)}) %copy-start.3) | copy-done | bytes 524312
  8.8 0.0 copy-start
  8.8 2.2 %front.1 = (f32[4,512,128]{2,1,0:T(8,128)S(1)}, f32[32,128]{1,0:T(8,128)S(1)}, f32[2,32,128]{2,1,0:T(8,128)S(1)}) custom-call(bf16[512,512]{1,0:T(8,128)(2,1)S(1)} %copy-done.1, bf16[512,512]{1,0:T(8,128)(2,1)S(1)} %copy-done.3, f32[9,512]{1,0:T(8,128)S(1)} %reshape.6.weight_ref), custom_call_target="tpu_custom_call" | custom-call | tf_op jit(solution)/shard_map/front/pallas_call | solution.py:431
  11.0 0.0 all-to-all-done.taps_ref
  11.0 0.0 copy-done
  11.0 0.7 deal.1
  11.7 0.0 copy-start.2
  11.7 0.0 copy-start.4
  11.7 0.0 copy-start.5
  11.7 30.1 %all_to_all.15.in_ref = bf16[32,72,128]{2,1,0:T(8,128)(2,1)S(1)} all-to-all(bf16[32,72,128]{2,1,0:T(8,128)(2,1)S(1)} %deal.1), channel_id=1, replica_groups=mesh['context'=32,'tensor'=8] {'context'}, dimensions={0} | all-to-all | bytes 1179648 | tf_op jit(solution)/shard_map/all_to_all | solution.py:476
  41.8 0.0 copy-done.2
  41.8 0.0 copy-done.4
  41.8 0.0 copy-done.5
  41.8 11.7 %conv.1 = (bf16[32,72,128]{2,1,0:T(8,128)(2,1)S(1)}, f32[512,512]{1,0:T(8,128)S(1)}, f32[512,512]{1,0:T(8,128)S(1)}) custom-call(bf16[32,72,128]{2,1,0:T(8,128)(2,1)S(1)} %all_to_all.15.in_ref, bf16[512,512]{1,0:T(8,128)(2,1)S(1)} %copy-done, bf16[512,512]{1,0:T(8,128)(2,1)S(1)} %copy-done.2, bf16[512,512]{1,0:T(8,128)(2,1)S(1)} %copy-done.4, ...), custom_call_target="tpu_custom_call" | custom-call | tf_op jit(solution)/shard_map/conv/pallas_call | solution.py:371
  53.5 22.8 %all_to_all.16.in_ref = bf16[32,72,128]{2,1,0:T(8,128)(2,1)S(1)} all-to-all(bf16[32,72,128]{2,1,0:T(8,128)(2,1)S(1)} %get-tuple-element.14), channel_id=1, replica_groups=mesh['context'=32,'tensor'=8] {'context'}, dimensions={0} | all-to-all | bytes 1179648 | tf_op jit(solution)/shard_map/all_to_all | solution.py:479
  76.3 1.5 %back.1 = bf16[512,512]{1,0:T(8,128)(2,1)} custom-call(bf16[32,72,128]{2,1,0:T(8,128)(2,1)S(1)} %all_to_all.16.in_ref, f32[512,512]{1,0:T(8,128)S(1)} %get-tuple-element.15.query_ref, f32[512,512]{1,0:T(8,128)S(1)} %get-tuple-element.16.base_ref), custom_call_target="tpu_custom_call" | custom-call | tf_op jit(solution)/shard_map/back/pallas_call | solution.py:444
  (1 shorter events, 0.0 us)
Async XLA Ops:
  0.0 6.7 %copy-start.6 = (f32[3,3,512]{2,1,0:T(4,128)S(1)}, f32[3,3,512]{2,1,0:T(4,128)}, u32[]{:S(2)}) copy-start(f32[3,3,512]{2,1,0:T(4,128)} %param.9) | copy-start | bytes 55300
  1.3 9.7 %all-to-all-start = ((f32[8,1,512]{2,1,0:T(1,128)}), f32[8,1,512]{2,1,0:T(1,128)S(1)}, u32[]{:S(2)}, u32[]{:S(2)}) async-start(f32[8,1,512]{2,1,0:T(1,128)} %broadcast_in_dim.12), calls=%async_computation | async-start | bytes 32768 | tf_op jit(solution)/shard_map/all_to_all | solution.py:464
  6.8 1.0 %copy-start.1 = (bf16[512,512]{1,0:T(8,128)(2,1)S(1)}, bf16[512,512]{1,0:T(8,128)(2,1)}, u32[]{:S(2)}) copy-start(bf16[512,512]{1,0:T(8,128)(2,1)} %key_ref.3) | copy-start | bytes 1572868
  7.8 1.0 %copy-start.3 = (bf16[512,512]{1,0:T(8,128)(2,1)S(1)}, bf16[512,512]{1,0:T(8,128)(2,1)}, u32[]{:S(2)}) copy-start(bf16[512,512]{1,0:T(8,128)(2,1)} %value_ref.3) | copy-start | bytes 1572868
  8.8 2.2 %copy-start = (bf16[512,512]{1,0:T(8,128)(2,1)S(1)}, bf16[512,512]{1,0:T(8,128)(2,1)}, u32[]{:S(2)}) copy-start(bf16[512,512]{1,0:T(8,128)(2,1)} %query_ref.3) | copy-start | bytes 1572868
  11.7 30.1 %copy-start.2 = (bf16[512,512]{1,0:T(8,128)(2,1)S(1)}, bf16[512,512]{1,0:T(8,128)(2,1)}, u32[]{:S(2)}) copy-start(bf16[512,512]{1,0:T(8,128)(2,1)} %key_ref.3) | copy-start | bytes 1572868
  11.7 30.1 %copy-start.4 = (bf16[512,512]{1,0:T(8,128)(2,1)S(1)}, bf16[512,512]{1,0:T(8,128)(2,1)}, u32[]{:S(2)}) copy-start(bf16[512,512]{1,0:T(8,128)(2,1)} %value_ref.3) | copy-start | bytes 1572868
  11.7 30.1 %copy-start.5 = (f32[512]{0:T(512)S(1)}, f32[512]{0:T(512)}, u32[]{:S(2)}) copy-start(f32[512]{0:T(512)} %param.10) | copy-start | bytes 6148

commit v6 on v5

--- a/solution.py
+++ b/solution.py
@@ -66,13 +66,13 @@
     return key_short * value_short
 
 
-def ends_of(refs, start, base):
+def ends_of(refs, start):
     shape = (TILE, TILE)
     lane = lax.broadcasted_iota(jnp.int32, shape, 1)
     place = lax.broadcasted_iota(jnp.int32, shape, 0)
     total = None
     for index, ref in enumerate(refs):
-        pick = (lane // 32 == base + index) & (place == start % TILE + lane % 32 // 16)
+        pick = (lane // 32 == index) & (place == start % TILE + lane % 32 // 16)
         part = jnp.dot(
             ref[:, start // TILE * TILE : start // TILE * TILE + TILE],
             pick.astype(jnp.bfloat16),
@@ -90,16 +90,12 @@
     return [part.reshape(ROWS, FILT, TILE).sum(axis=0) for part in spread]
 
 
-def front_kernel(key_ref, value_ref, weight_ref, coded_ref, scale_ref, ends_ref):
+def front_kernel(key_ref, value_ref, weight_ref, coded_ref, scale_ref):
     length = key_ref.shape[1]
-    refs = (key_ref, value_ref)
     lane = lax.broadcasted_iota(jnp.int32, (TILE, length), 1)
-    both = [ends_of(refs, start, 0) for start in (0, length - 2)]
     for step in range(key_ref.shape[0] // TILE):
         rows = slice(step * TILE, (step + 1) * TILE)
         dests = slice(step * FILT, (step + 1) * FILT)
-        for which, part in enumerate(ends_rows(both, step)):
-            ends_ref[which, dests, :] = part
         side = side_columns([weight_ref[:, rows]])
         product = jnp.where(lane < 2, 0.0, product_of(key_ref, value_ref, side, rows))
         scale = scale_of(jnp.max(jnp.abs(product), axis=1, keepdims=True))
@@ -109,8 +105,9 @@
         scale_ref[dests, :] = to_lanes(scale)
 
 
-def deal_kernel(coded_ref, scale_ref, ends_ref, query_ref, taps_ref, out_ref):
-    both = [ends_of((query_ref,), start, 2) for start in (0, query_ref.shape[1] - 2)]
+def deal_kernel(coded_ref, scale_ref, key_ref, value_ref, query_ref, taps_ref, out_ref):
+    refs = (key_ref, value_ref, query_ref)
+    both = [ends_of(refs, start) for start in (0, query_ref.shape[1] - 2)]
     row = lax.broadcasted_iota(jnp.int32, (8, TILE), 0)
     tails = []
     for filt in range(FILT):
@@ -131,9 +128,9 @@
             part = coded_ref[block, rows, :]
             out_ref[dest, block * ROWS : (block + 1) * ROWS, :] = part.astype(jnp.bfloat16)
         tail = jnp.where(row == 4, scale_ref[dest : dest + 1, :], tails[filt])
-        ends = ends_ref[0, dest : dest + 1, :] + late[0][filt : filt + 1, :]
+        ends = late[0][filt : filt + 1, :]
         tail = jnp.where(row == 6, ends, tail)
-        ends = ends_ref[1, dest : dest + 1, :] + late[1][filt : filt + 1, :]
+        ends = late[1][filt : filt + 1, :]
         tail = jnp.where(row == 7, ends, tail)
         out_ref[dest, 64:72, :] = tail.astype(jnp.bfloat16)
 
@@ -467,12 +464,11 @@
     outs = [
         ((4, rows, TILE), jnp.float32),
         ((count, TILE), jnp.float32),
-        ((2, count, TILE), jnp.float32),
     ]
     streams = (key_proj, value_proj)
-    coded, scales, ends = whole_call(front_kernel, "front", outs, *streams, weight)
+    coded, scales = whole_call(front_kernel, "front", outs, *streams, weight)
     outs = [((count, CHUNK, TILE), jnp.bfloat16)]
-    (chunks,) = whole_call(deal_kernel, "deal", outs, coded, scales, ends, query_proj, taps)
+    (chunks,) = whole_call(deal_kernel, "deal", outs, coded, scales, *streams, query_proj, taps)
     chunks = lax.all_to_all(chunks, "context", 0, 0, tiled=True)
     streams = (query_proj, key_proj, value_proj)
     chunks, query_short, base = conv(chunks, streams, weight, skip)

time: 78.3 us -> 79.4 us (1.014)
  local copies, waits for them, and re-layouts: 3.42 us -> 4.45 us
    unnamed x14 -> x16, local copies, waits for them, and re-layouts: 2.1 us -> 3.14 us
where the time goes in v6:
time: 79.4 us; the launch traced here: 79 us
  blocking collectives  52.9 us (67%)
  Pallas kernels  15.9 us (20%)
  starting transfers between devices  5.43 us (7%)
  local copies, waits for them, and re-layouts  4.45 us (6%)
    all_to_all x2, blocking collectives, local(): chunks = lax.all_to_all(chunks, 'context', 0, 0, tiled=True)  52.9 us
    pallas_call x1, Pallas kernels, conv(): pl.pallas_call(conv_kernel, in_specs=[whole] * 6, out_specs=[whole] * 3,...  11.6 us
    all_to_all x1, starting transfers between devices, local(): taps = lax.all_to_all(taps, 'tensor', 0, 0, tiled=True)  5.43 us
    unnamed x16, local copies, waits for them, and re-layouts  3.14 us
    pallas_call x2, Pallas kernels, whole_call(): pl.pallas_call(kernel, in_specs=[WHOLE] * len(operands), out_specs=[WHOLE...  2.79 us
  transfers between devices with their start and end apart: 1, of which 0 were waited for; matrix products, arithmetic and copies ran while one was open for 0% of the time, Pallas kernels for 3%

profile of v6, /device:TPU:8, one launch (start us, length us, event | category | flops | bytes accessed | tf_op | source)
XLA Modules:
  0.0 79.0 jit_solution(1957241727435600920)
XLA Ops:
  0.0 0.0 copy-start.7
  0.0 1.3 %broadcast_in_dim.12 = f32[8,1,512]{2,1,0:T(1,128)} broadcast(f32[512]{0:T(512)} %bitcast.3), dimensions={2} | broadcast | bytes 18432 | tf_op jit(solution)/shard_map/broadcast_in_dim | solution.py:460
  1.3 5.4 %all-to-all-start = ((f32[8,1,512]{2,1,0:T(1,128)}), f32[8,1,512]{2,1,0:T(1,128)S(1)}, u32[]{:S(2)}, u32[]{:S(2)}) async-start(f32[8,1,512]{2,1,0:T(1,128)} %broadcast_in_dim.12), calls=%async_computation | async-start | bytes 32768 | tf_op jit(solution)/shard_map/all_to_all | solution.py:461
  6.7 0.0 copy-done.7
  6.8 0.0 copy-start
  6.8 1.0 %copy-done = bf16[512,512]{1,0:T(8,128)(2,1)S(1)} copy-done((bf16[512,512]{1,0:T(8,128)(2,1)S(1)}, bf16[512,512]{1,0:T(8,128)(2,1)}, u32[]{:S(2)}) %copy-start) | copy-done | bytes 524312
  7.8 0.0 copy-start.2
  7.8 1.0 %copy-done.2 = bf16[512,512]{1,0:T(8,128)(2,1)S(1)} copy-done((bf16[512,512]{1,0:T(8,128)(2,1)S(1)}, bf16[512,512]{1,0:T(8,128)(2,1)}, u32[]{:S(2)}) %copy-start.2) | copy-done | bytes 524312
  8.8 0.0 copy-start.1
  8.8 0.0 copy-start.3
  8.8 2.1 %front.1 = (f32[4,512,128]{2,1,0:T(8,128)S(1)}, f32[32,128]{1,0:T(8,128)S(1)}) custom-call(bf16[512,512]{1,0:T(8,128)(2,1)S(1)} %copy-done, bf16[512,512]{1,0:T(8,128)(2,1)S(1)} %copy-done.2, f32[9,512]{1,0:T(8,128)S(1)} %reshape.6.weight_ref), custom_call_target="tpu_custom_call" | custom-call | tf_op jit(solution)/shard_map/front/pallas_call | solution.py:428
  11.0 0.0 all-to-all-done.taps_ref
  11.0 0.0 copy-done.1
  11.0 0.0 copy-done.3
  11.0 0.0 copy-start.4
  11.0 1.0 %copy-done.4 = bf16[512,512]{1,0:T(8,128)(2,1)S(1)} copy-done((bf16[512,512]{1,0:T(8,128)(2,1)S(1)}, bf16[512,512]{1,0:T(8,128)(2,1)}, u32[]{:S(2)}) %copy-start.4) | copy-done | bytes 524312
  12.0 0.7 deal.1
  12.7 0.0 copy-start.5
  12.7 0.0 copy-start.6
  12.7 30.1 %all_to_all.15.in_ref = bf16[32,72,128]{2,1,0:T(8,128)(2,1)S(1)} all-to-all(bf16[32,72,128]{2,1,0:T(8,128)(2,1)S(1)} %deal.1), channel_id=1, replica_groups=mesh['context'=32,'tensor'=8] {'context'}, dimensions={0} | all-to-all | bytes 1179648 | tf_op jit(solution)/shard_map/all_to_all | solution.py:472
  42.8 0.0 copy-done.5
  42.8 0.0 copy-done.6
  42.8 11.6 %conv.1 = (bf16[32,72,128]{2,1,0:T(8,128)(2,1)S(1)}, f32[512,512]{1,0:T(8,128)S(1)}, f32[512,512]{1,0:T(8,128)S(1)}) custom-call(bf16[32,72,128]{2,1,0:T(8,128)(2,1)S(1)} %all_to_all.15.in_ref, bf16[512,512]{1,0:T(8,128)(2,1)S(1)} %copy-done.5, bf16[512,512]{1,0:T(8,128)(2,1)S(1)} %copy-done.1, bf16[512,512]{1,0:T(8,128)(2,1)S(1)} %copy-done.3, ...), custom_call_target="tpu_custom_call" | custom-call | tf_op jit(solution)/shard_map/conv/pallas_call | solution.py:368
  54.5 22.8 %all_to_all.16.in_ref = bf16[32,72,128]{2,1,0:T(8,128)(2,1)S(1)} all-to-all(bf16[32,72,128]{2,1,0:T(8,128)(2,1)S(1)} %get-tuple-element.12), channel_id=1, replica_groups=mesh['context'=32,'tensor'=8] {'context'}, dimensions={0} | all-to-all | bytes 1179648 | tf_op jit(solution)/shard_map/all_to_all | solution.py:475
  77.3 1.5 %back.1 = bf16[512,512]{1,0:T(8,128)(2,1)} custom-call(bf16[32,72,128]{2,1,0:T(8,128)(2,1)S(1)} %all_to_all.16.in_ref, f32[512,512]{1,0:T(8,128)S(1)} %get-tuple-element.13.query_ref, f32[512,512]{1,0:T(8,128)S(1)} %get-tuple-element.14.base_ref), custom_call_target="tpu_custom_call" | custom-call | tf_op jit(solution)/shard_map/back/pallas_call | solution.py:441
  (1 shorter events, 0.0 us)
Async XLA Ops:
  0.0 6.7 %copy-start.7 = (f32[3,3,512]{2,1,0:T(4,128)S(1)}, f32[3,3,512]{2,1,0:T(4,128)}, u32[]{:S(2)}) copy-start(f32[3,3,512]{2,1,0:T(4,128)} %param.9) | copy-start | bytes 55300
  1.3 9.7 %all-to-all-start = ((f32[8,1,512]{2,1,0:T(1,128)}), f32[8,1,512]{2,1,0:T(1,128)S(1)}, u32[]{:S(2)}, u32[]{:S(2)}) async-start(f32[8,1,512]{2,1,0:T(1,128)} %broadcast_in_dim.12), calls=%async_computation | async-start | bytes 32768 | tf_op jit(solution)/shard_map/all_to_all | solution.py:461
  6.8 1.0 %copy-start = (bf16[512,512]{1,0:T(8,128)(2,1)S(1)}, bf16[512,512]{1,0:T(8,128)(2,1)}, u32[]{:S(2)}) copy-start(bf16[512,512]{1,0:T(8,128)(2,1)} %key_ref.5) | copy-start | bytes 1572868
  7.8 1.0 %copy-start.2 = (bf16[512,512]{1,0:T(8,128)(2,1)S(1)}, bf16[512,512]{1,0:T(8,128)(2,1)}, u32[]{:S(2)}) copy-start(bf16[512,512]{1,0:T(8,128)(2,1)} %value_ref.5) | copy-start | bytes 1572868
  8.8 2.1 %copy-start.1 = (bf16[512,512]{1,0:T(8,128)(2,1)S(1)}, bf16[512,512]{1,0:T(8,128)(2,1)}, u32[]{:S(2)}) copy-start(bf16[512,512]{1,0:T(8,128)(2,1)} %key_ref.5) | copy-start | bytes 1572868
  8.8 2.1 %copy-start.3 = (bf16[512,512]{1,0:T(8,128)(2,1)S(1)}, bf16[512,512]{1,0:T(8,128)(2,1)}, u32[]{:S(2)}) copy-start(bf16[512,512]{1,0:T(8,128)(2,1)} %value_ref.5) | copy-start | bytes 1572868
  11.0 1.0 %copy-start.4 = (bf16[512,512]{1,0:T(8,128)(2,1)S(1)}, bf16[512,512]{1,0:T(8,128)(2,1)}, u32[]{:S(2)}) copy-start(bf16[512,512]{1,0:T(8,128)(2,1)} %query_ref.3) | copy-start | bytes 1572868
  12.7 30.1 %copy-start.5 = (bf16[512,512]{1,0:T(8,128)(2,1)S(1)}, bf16[512,512]{1,0:T(8,128)(2,1)}, u32[]{:S(2)}) copy-start(bf16[512,512]{1,0:T(8,128)(2,1)} %query_ref.3) | copy-start | bytes 1572868
  12.7 30.1 %copy-start.6 = (f32[512]{0:T(512)S(1)}, f32[512]{0:T(512)}, u32[]{:S(2)}) copy-start(f32[512]{0:T(512)} %param.10) | copy-start | bytes 6148
